TPU v7x, 128 devices: a whole 4x4x4 slice. The times are simulated.
128 devices in a mesh: row: 16 (over z_hi, x, core), col: 8 (over z_lo, y).
Axes of the slice: x: 4, y: 4, z: 4 (z_hi: 2, z_lo: 2; z = z_hi * 2 + z_lo), core: 2. Of those that a mesh axis runs over, the one named last changes fastest.
Arguments:
- pair: bfloat16 [512, 512, 128], P('row', 'col'), may hold values from -6 to 6
- in_gain: float32 [128], replicated, may hold values from 0.1 to 1.9
- in_bias: float32 [128], replicated, may hold values from -3 to 3
- a_gate: bfloat16 [128, 128], replicated, may hold values from -0.5 to 0.5
- a_proj: bfloat16 [128, 128], replicated, may hold values from -0.5 to 0.5
- b_gate: bfloat16 [128, 128], replicated, may hold values from -0.5 to 0.5
- b_proj: bfloat16 [128, 128], replicated, may hold values from -0.5 to 0.5
- out_gate: bfloat16 [128, 128], replicated, may hold values from -0.5 to 0.5
- mid_gain: float32 [128], replicated, may hold values from 0.1 to 1.9
- mid_bias: float32 [128], replicated, may hold values from -3 to 3
- out_proj: bfloat16 [128, 128], replicated, may hold values from -0.5 to 0.5
Outputs:
- update: bfloat16 [512, 512, 128], P('row', 'col')
All inputs are finite; a program needn't handle non-finite values.
Results may differ from a plain program's by a relative error of at most 0.0054.
Values may be sent and summed in bfloat16 or wider, within the bound.
No kernel may reach another device: no remote copies, remote signals or barrier semaphores. Data moves between devices by JAX's collectives and lax.ppermute only.
A program may use at most 128 MiB of HBM per device.

v0:
```python
import jax
import jax.numpy as jnp
from jax import lax
from jax.sharding import PartitionSpec as P


def spread(block, axis, source):
    block = jnp.where(lax.axis_index(axis) == source, block, jnp.zeros_like(block))
    return lax.psum(block, axis)


def layer_norm(values, gain, bias):
    mean = jnp.mean(values, axis=-1, keepdims=True)
    centered = values - mean
    variance = jnp.mean(centered * centered, axis=-1, keepdims=True)
    return centered * lax.rsqrt(variance + 1e-05) * gain + bias


def per_device(
    pair, in_gain, in_bias, a_gate, a_proj, b_gate, b_proj, out_gate, mid_gain, mid_bias, out_proj
):
    rows_here, cols_here, chans = pair.shape
    hidden = a_gate.shape[1]
    normed = layer_norm(pair.astype(jnp.float32), in_gain, in_bias).astype(jnp.bfloat16)
    weights = jnp.concatenate([a_gate, a_proj, b_gate, b_proj, out_gate], axis=1)
    projected = jnp.dot(
        normed.reshape(rows_here * cols_here, chans), weights, preferred_element_type=jnp.float32
    )
    left = (jax.nn.sigmoid(projected[:, :hidden]) * projected[:, hidden : 2 * hidden]).astype(
        jnp.bfloat16
    )
    right = (
        jax.nn.sigmoid(projected[:, 2 * hidden : 3 * hidden])
        * projected[:, 3 * hidden : 4 * hidden]
    ).astype(jnp.bfloat16)
    gate = jax.nn.sigmoid(projected[:, 4 * hidden :]).reshape(rows_here, cols_here, chans)
    left = left.reshape(rows_here, cols_here, hidden)
    right = right.reshape(rows_here, cols_here, hidden)
    row_count = lax.axis_size("row")
    col_count = lax.axis_size("col")
    ratio = row_count // col_count
    first_root = ratio * lax.axis_index("col")
    left_panel, right_panel = (
        lax.all_gather(left, "col", axis=1, tiled=True),
        lax.all_gather(right, "col", axis=1, tiled=True),
    )
    blocks = []
    for offset in range(ratio):
        blocks.append(spread(right_panel, "row", first_root + offset))
    mirrored = jnp.concatenate(blocks, axis=0)
    triangle = jnp.einsum("ikc,jkc->ijc", left_panel, mirrored, preferred_element_type=jnp.float32)
    mixed = layer_norm(triangle, mid_gain, mid_bias).astype(jnp.bfloat16)
    output = jnp.dot(
        mixed.reshape(rows_here * cols_here, hidden), out_proj, preferred_element_type=jnp.float32
    )
    return (gate * output.reshape(rows_here, cols_here, chans)).astype(jnp.bfloat16)


def solution(mesh):
    in_specs = (P("row", "col", None), P(), P(), P(), P(), P(), P(), P(), P(), P(), P())
    out_specs = P("row", "col", None)
    return jax.shard_map(
        per_device, mesh=mesh, in_specs=in_specs, out_specs=out_specs, check_vma=False
    )
```

profile of v0, /device:TPU:0, one launch (start us, length us, event | category | flops | bytes accessed | tf_op | source)
XLA Modules:
  0.0 307.3 jit_solution(1612785263548689200)
XLA Ops:
  6.5 0.0 copy-start
  6.5 0.0 all-gather.3.cloned.1.call-start
  6.5 1.4 convert_reduce_fusion
  7.9 1.7 fusion.7
  9.7 0.8 constant_dynamic-update-slice_fusion.4
  10.4 0.8 constant_dynamic-update-slice_fusion.3
  11.2 0.8 constant_dynamic-update-slice_fusion.2
  12.0 0.8 constant_dynamic-update-slice_fusion.1
  12.7 0.8 constant_dynamic-update-slice_fusion
  13.5 1.7 fusion.10
  15.2 0.8 fusion.25
  16.0 0.8 fusion.15
  16.8 1.2 copy.15
  18.0 0.0 all-gather.3.cloned.1.call-update
  18.0 0.0 all-gather.5.cloned.1.call-start
  18.1 1.1 copy.18
  19.2 0.0 all-gather.5.cloned.1.call-update
  19.2 0.0 all-reduce.3.cloned.1.call-start
  19.3 54.0 %all-gather.3.cloned.1.call-done = bf16[32,512,128]{2,0,1:T(8,128)(2,1)} async-done(((bf16[32,64,128]{2,0,1:T(8,128)(2,1)}), bf16[32,512,128]{2,0,1:T(8,128)(2,1)}) %all-gather.3.cloned.1.call-update) | async-done | bytes 4194320 | tf_op jit(solution)/shard_map/all_gather | solution.py:45
  73.3 8.6 %copy.16 = bf16[32,512,128]{1,0,2:T(8,128)(2,1)} copy(bf16[32,512,128]{2,0,1:T(8,128)(2,1)} %all-gather.3.cloned.1.call-done) | data formatting | bytes 8388608 | tf_op jit(solution)/shard_map/all_gather | solution.py:45
  81.9 6.0 %broadcast_select_fusion.1 = (bf16[32,512,128]{1,0,2:T(8,128)(2,1)}, bf16[32,512,128]{1,0,2:T(8,128)(2,1)}) fusion(bf16[32,512,128]{1,0,2:T(8,128)(2,1)} %copy.16, pred[]{:T(512)S(6)} %eq.6, pred[]{:T(512)S(6)} %eq.7), kind=kLoop, calls=%fused_computation.5 | loop fusion | flops 4194304 | bytes 12582914 | tf_op jit(solution)/shard_map/jit(_where)/select_n | solution.py:8
  87.9 0.0 all-reduce.3.cloned.1.call-update
  88.0 38.4 %all-gather.5.cloned.1.call-done = bf16[32,512,128]{2,0,1:T(8,128)(2,1)} async-done(((bf16[32,64,128]{2,0,1:T(8,128)(2,1)}), bf16[32,512,128]{2,0,1:T(8,128)(2,1)}) %all-gather.5.cloned.1.call-update) | async-done | bytes 4194320 | tf_op jit(solution)/shard_map/all_gather | solution.py:44
  126.4 8.6 %copy.19 = bf16[32,512,128]{1,0,2:T(8,128)(2,1)} copy(bf16[32,512,128]{2,0,1:T(8,128)(2,1)} %all-gather.5.cloned.1.call-done) | data formatting | bytes 8388608 | tf_op jit(solution)/shard_map/all_gather | solution.py:44
  135.0 156.6 %all-reduce.3.cloned.1.call-done = (bf16[32,512,128]{1,0,2:T(8,128)(2,1)}, bf16[32,512,128]{1,0,2:T(8,128)(2,1)}) async-done(((bf16[32,512,128]{1,0,2:T(8,128)(2,1)}, bf16[32,512,128]{1,0,2:T(8,128)(2,1)}), (bf16[32,512,128]{1,0,2:T(8,128)(2,1)}, bf16[32,512,128]{1,0,2:T(8,128)(2,1)})) %all-reduce.3.cloned.1.call-update) | async-done | bytes 8388624 | tf_op jit(solution)/shard_map/psum | solution.py:9
  291.6 0.0 copy-start.1
  291.6 0.0 copy-start.2
  291.6 7.0 %bitcast_reduce_fusion = (f32[32,64]{1,0:T(8,128)S(1)}, f32[128,64,32]{1,2,0:T(8,128)S(1)}) fusion(bf16[32,512,128]{1,0,2:T(8,128)(2,1)} %copy.19, bf16[32,512,128]{1,0,2:T(8,128)(2,1)} %get-tuple-element.5, bf16[32,512,128]{1,0,2:T(8,128)(2,1)} %get-tuple-element.6), kind=kOutput, calls=%fused_computation.7 | convolution fusion | flops 285472768 | bytes 13639680 | tf_op jit(solution)/shard_map/ikc,jkc->ijc/dot_general | solution.py:51
  298.6 0.3 multiply_reduce_fusion
  299.0 0.0 copy-done.1
  299.0 0.0 copy-done.2
  299.0 0.4 add_convert_fusion
  299.4 0.0 copy-done
  299.4 1.3 fusion.4
  (4 shorter events, 0.0 us)
Async XLA Ops:
  6.5 292.9 %copy-start = (bf16[128,128]{1,0:T(8,128)(2,1)S(1)}, bf16[128,128]{1,0:T(8,128)(2,1)}, u32[]{:S(2)}) copy-start(bf16[128,128]{1,0:T(8,128)(2,1)} %param.21) | copy-start | bytes 98308
  6.5 66.8 %all-gather.3.cloned.1.call-start = ((), (), s32[]{:S(2)}) async-start(), calls=%async_computation | async-start | bytes 4718592 | tf_op jit(solution)/shard_map/all_gather | solution.py:45
  18.0 108.3 %all-gather.5.cloned.1.call-start = ((), (), s32[]{:S(2)}) async-start(), calls=%async_computation.1 | async-start | bytes 4718592 | tf_op jit(solution)/shard_map/all_gather | solution.py:44
  19.2 272.4 %all-reduce.3.cloned.1.call-start = ((), (), s32[]{:S(2)}) async-start(), calls=%async_computation.2 | async-start | bytes 16777216 | tf_op jit(solution)/shard_map/psum | solution.py:9
  291.6 7.3 %copy-start.1 = (f32[128]{0:T(128)S(1)}, f32[128]{0:T(128)}, u32[]{:S(2)}) copy-start(f32[128]{0:T(128)} %param.20) | copy-start | bytes 1540
  291.6 7.4 %copy-start.2 = (f32[128]{0:T(128)S(1)}, f32[128]{0:T(128)}, u32[]{:S(2)}) copy-start(f32[128]{0:T(128)} %param.19) | copy-start | bytes 1540
Sparse Core Ops, SparseCore 0:
  18.2 55.1 all-gather.2
  75.0 51.3 all-gather.4
  128.9 162.6 all-reduce.2
where the time goes:
time: 308 us; the launch traced here: 307 us
  waiting for transfers between devices  249 us (81%)
  local copies, waits for them, and re-layouts  23.4 us (8%)
  between operations  13.2 us (4%)
  other arithmetic  12.3 us (4%)
  matrix products  9.13 us (3%)
    psum x1, waiting for transfers between devices, spread(): return lax.psum(block, axis)  157 us
    all_gather x1, waiting for transfers between devices, per_device(): lax.all_gather(right, 'col', axis=1, tiled=True)  54 us
    all_gather x1, waiting for transfers between devices, per_device(): lax.all_gather(left, 'col', axis=1, tiled=True)  38.4 us
    all_gather x1, local copies, waits for them, and re-layouts, per_device(): lax.all_gather(left, 'col', axis=1, tiled=True)  8.63 us
    all_gather x1, local copies, waits for them, and re-layouts, per_device(): lax.all_gather(right, 'col', axis=1, tiled=True)  8.59 us
    dot_general x1, matrix products, per_device(): jnp.einsum('ikc,jkc->ijc', left_panel, mirrored, preferred_element_type=j...  6.98 us
  transfers between devices with their start and end apart: 3, of which 3 were waited for; matrix products, arithmetic and copies ran while one was open for 8% of the time, Pallas kernels for 0%

commit v1 on v0

v1 whole, which is shorter than its diff:
```python
import jax
import jax.numpy as jnp
from jax import lax
from jax.experimental import pallas as pl
from jax.experimental.pallas import tpu as pltpu
from jax.sharding import PartitionSpec as P

BF16, F32 = jnp.bfloat16, jnp.float32
EPS = 1e-05
BOTH = ("row", "col")


def sigmoid(x):
    return 0.5 + 0.5 * jnp.tanh(0.5 * x)


def identity(size):
    return (
        lax.broadcasted_iota(jnp.int32, (size, size), 0)
        == lax.broadcasted_iota(jnp.int32, (size, size), 1)
    ).astype(BF16)


def dot(a, b, contract):
    return lax.dot_general(a, b, ((contract[:1], contract[1:]), ((), ())), preferred_element_type=F32)


def column(vector, width):
    return jnp.broadcast_to(vector, (width, vector.shape[1])).T


def norm(values, axis):
    mean = jnp.mean(values, axis=axis, keepdims=True)
    centered = values - mean
    variance = jnp.mean(centered * centered, axis=axis, keepdims=True)
    return centered * lax.rsqrt(variance + EPS)


def operands_kernel(pair_ref, gain_ref, bias_ref, ag_ref, ap_ref, bg_ref, bp_ref, out_ref, wide_ref):
    rows, cols, chans = pair_ref.shape
    half = rows // 2
    tiles = 2 * half
    eye = identity(chans)
    gain, bias = column(gain_ref[...], 2 * cols), column(bias_ref[...], 2 * cols)
    weights = [ref[...].T for ref in (ag_ref, ap_ref, bg_ref, bp_ref)]
    for s in range(half):
        block = jnp.concatenate([pair_ref[s], pair_ref[half + s]], axis=0)
        turned = dot(eye, block, (1, 1))
        normed = (norm(turned, 0) * gain + bias).astype(BF16)
        a_gate, a_proj, b_gate, b_proj = (dot(w, normed, (1, 0)) for w in weights)
        wide_ref[pl.ds(s, chans, stride=tiles), :] = sigmoid(a_gate) * a_proj
        wide_ref[pl.ds(half + s, chans, stride=tiles), :] = sigmoid(b_gate) * b_proj
    out_ref[...] = wide_ref[...].astype(BF16).reshape(out_ref.shape)


def gate_kernel(pair_ref, gain_ref, bias_ref, weight_ref, out_ref):
    rows, cols, chans = pair_ref.shape
    values = pair_ref[...].reshape(rows * cols, chans).astype(F32)
    normed = (norm(values, 1) * gain_ref[...] + bias_ref[...]).astype(BF16)
    out_ref[...] = sigmoid(dot(normed, weight_ref[...], (1, 0))).reshape(out_ref.shape)


def product_kernel(in_ref, out_ref, left_ref, right_ref):
    row_count, col_count, lanes = in_ref.shape[0], in_ref.shape[1], in_ref.shape[3]
    tile = in_ref.shape[2] // 2
    cols = lanes // 2
    groups = row_count * tile
    for m in range(col_count // 2):
        for which, ref in ((0, left_ref), (1, right_ref)):
            part = pl.ds(which * tile, tile)
            even = in_ref[:, 2 * m, part, :]
            odd = in_ref[:, 2 * m + 1, part, :]
            for h in range(2):
                ref[:, h, :, m * lanes : (m + 1) * lanes] = jnp.concatenate(
                    [even[:, :, h * cols : (h + 1) * cols], odd[:, :, h * cols : (h + 1) * cols]], axis=2
                )
    depth = right_ref.shape[3]
    right = right_ref[...].reshape(2 * groups, depth)
    products = [
        dot(left_ref[:, h].reshape(groups, depth), right, (1, 1)).astype(BF16).reshape(row_count, tile, 2 * groups)
        for h in range(2)
    ]
    for m in range(col_count // 2):
        first, second = (p[:, :, m * lanes : (m + 1) * lanes] for p in products)
        for odd in range(2):
            cut = slice(odd * cols, (odd + 1) * cols)
            out_ref[:, 2 * m + odd] = jnp.concatenate(
                [first[:, :, cut], second[:, :, cut]], axis=2
            )


def update_kernel(in_ref, gate_ref, gain_ref, bias_ref, weight_ref, out_ref, wide_ref):
    chans, half, lanes = in_ref.shape
    cols = lanes // 2
    gain, bias = column(gain_ref[...], lanes), column(bias_ref[...], lanes)
    wide_ref[...] = norm(in_ref[...].astype(F32), 0).reshape(wide_ref.shape)
    for s in range(half):
        mixed = (wide_ref[pl.ds(s, chans, stride=half), :] * gain + bias).astype(BF16)
        output = dot(mixed, weight_ref[...], (0, 0))
        out_ref[s] = (gate_ref[s] * output[:cols]).astype(BF16)
        out_ref[half + s] = (gate_ref[half + s] * output[cols:]).astype(BF16)


VMEM_LIMIT = 48 * 2**20


def call(kernel, out, scratch=(), flops=0):
    return pl.pallas_call(
        kernel,
        out_shape=out,
        scratch_shapes=list(scratch),
        compiler_params=pltpu.CompilerParams(vmem_limit_bytes=VMEM_LIMIT),
        cost_estimate=pl.CostEstimate(flops=flops, bytes_accessed=2**20, transcendentals=2**18),
    )


def per_device(
    pair, in_gain, in_bias, a_gate, a_proj, b_gate, b_proj, out_gate, mid_gain, mid_bias, out_proj
):
    rows, cols, chans = pair.shape
    hidden = a_gate.shape[1]
    row_count, col_count = lax.axis_size("row"), lax.axis_size("col")
    half, lanes = rows // 2, 2 * cols
    gain, bias = in_gain[None, :], in_bias[None, :]
    operands = call(
        operands_kernel,
        jax.ShapeDtypeStruct((hidden, 2 * half, lanes), BF16),
        [pltpu.VMEM((hidden * 2 * half, lanes), F32)],
        2 * rows * cols * chans * 4 * hidden,
    )(pair, gain, bias, a_gate, a_proj, b_gate, b_proj)
    channel = lax.all_to_all(operands, BOTH, 0, 0, tiled=True)
    gate = call(gate_kernel, jax.ShapeDtypeStruct(pair.shape, F32), (), 2 * rows * cols * chans * chans)(
        pair, gain, bias, out_gate
    )
    count, depth = row_count * half, col_count * cols
    triangle = call(
        product_kernel,
        jax.ShapeDtypeStruct((row_count, col_count, half, lanes), BF16),
        [pltpu.VMEM((row_count, 2, half, depth), BF16), pltpu.VMEM((row_count, 2, half, depth), BF16)],
        8 * count * count * depth,
    )(channel.reshape(row_count, col_count, 2 * half, lanes))
    triangle = lax.all_to_all(triangle.reshape(operands.shape[0], half, lanes), BOTH, 0, 0, tiled=True)
    return call(
        update_kernel,
        jax.ShapeDtypeStruct(pair.shape, BF16),
        [pltpu.VMEM((hidden * half, lanes), F32)],
        2 * rows * cols * hidden * chans,
    )(triangle, gate, mid_gain[None, :], mid_bias[None, :], out_proj)


def solution(mesh):
    in_specs = (P("row", "col", None), P(), P(), P(), P(), P(), P(), P(), P(), P(), P())
    return jax.shard_map(
        per_device, mesh=mesh, in_specs=in_specs, out_specs=P("row", "col", None), check_vma=False
    )
```

time: 308 us -> 63.5 us (0.21)
  waiting for transfers between devices: 249 us -> 12.6 us
  blocking collectives: 0 us -> 30 us
  local copies, waits for them, and re-layouts: 23.4 us -> 5.42 us
  between operations: 13.2 us -> 0.06 us
  other arithmetic: 12.3 us -> 0 us
  Pallas kernels: 0 us -> 9.96 us
  matrix products: 9.13 us -> 0 us
  starting transfers between devices: 0.09 us -> 4.75 us
    psum x1 -> x0, waiting for transfers between devices: 157 us -> none  [spread(): return lax.psum(block, axis)]
    all_gather x2 -> x0, waiting for transfers between devices: 92.5 us -> none  [the longest x1 54 us: per_device(): lax.all_gather(right, 'col', axis=1, tiled=True)]
    all_to_all x0 -> x1, blocking collectives: none -> 30 us  [per_device(): channel = lax.all_to_all(operands, BOTH, 0, 0, tiled=True)]
    all_gather x2 -> x0, local copies, waits for them, and re-layouts: 17.2 us -> none  [the longest x1 8.63 us: per_device(): lax.all_gather(left, 'col', axis=1, tiled=True)]
    all_to_all x0 -> x1, waiting for transfers between devices: none -> 12.6 us  [per_device(): lax.all_to_all(triangle.reshape(operands.shape[0], half, lanes), BOTH, 0,...]
    pallas_call x0 -> x4, Pallas kernels: none -> 9.96 us  [the longest x1 5.89 us: per_device(): call(operands_kernel, jax.ShapeDtypeStruct((hidden, 2 * half, lanes), BF1...]
    dot_general x3 -> x0, matrix products: 9.13 us -> none  [the longest x1 6.98 us: per_device(): jnp.einsum('ikc,jkc->ijc', left_panel, mirrored, preferred_element_type=j...]
    select_n x1 -> x0, other arithmetic: 6.01 us -> none  [spread(): jnp.where(lax.axis_index(axis) == source, block, jnp.zeros_like(block))]
  transfers between devices with their start and end apart: 3 -> 1, of which waited for: 3 -> 1; matrix products, arithmetic and copies ran while one was open for 8% -> 0% of each run, Pallas kernels for 0% -> 1%
where the time goes in v1:
time: 63.5 us; the launch traced here: 62.8 us
  blocking collectives  30 us (47%)
  waiting for transfers between devices  12.6 us (20%)
  Pallas kernels  9.96 us (16%)
  local copies, waits for them, and re-layouts  5.42 us (9%)
  starting transfers between devices  4.75 us (7%)
    all_to_all x1, blocking collectives, per_device(): channel = lax.all_to_all(operands, BOTH, 0, 0, tiled=True)  30 us
    all_to_all x1, waiting for transfers between devices, per_device(): lax.all_to_all(triangle.reshape(operands.shape[0], half, lanes), BOTH, 0,...  12.6 us
    pallas_call x1, Pallas kernels, per_device(): call(operands_kernel, jax.ShapeDtypeStruct((hidden, 2 * half, lanes), BF1...  5.89 us
    unnamed x24, local copies, waits for them, and re-layouts  5.42 us
    all_to_all x1, starting transfers between devices, per_device(): lax.all_to_all(triangle.reshape(operands.shape[0], half, lanes), BOTH, 0,...  4.75 us
    pallas_call x1, Pallas kernels, per_device(): call(update_kernel, jax.ShapeDtypeStruct(pair.shape, BF16), [pltpu.VMEM((...  1.73 us
    pallas_call x1, Pallas kernels, per_device(): call(product_kernel, jax.ShapeDtypeStruct((row_count, col_count, half, la...  1.52 us
  transfers between devices with their start and end apart: 1, of which 1 were waited for; matrix products, arithmetic and copies ran while one was open for 0% of the time, Pallas kernels for 1%

profile of v1, /device:TPU:0, one launch (start us, length us, event | category | flops | bytes accessed | tf_op | source)
XLA Modules:
  0.0 62.8 jit_solution(9320106590271087062)
XLA Ops:
  0.0 0.0 copy-start.8
  0.0 0.0 copy-start.9
  0.0 0.7 %copy-done.8 = f32[128]{0:T(128)S(1)} copy-done((f32[128]{0:T(128)S(1)}, f32[128]{0:T(128)}, u32[]{:S(2)}) %copy-start.8) | copy-done | bytes 536
  0.7 0.0 copy-done.9
  0.7 0.0 copy-start
  0.7 1.0 %copy-done = bf16[32,64,128]{2,1,0:T(8,128)(2,1)S(1)} copy-done((bf16[32,64,128]{2,1,0:T(8,128)(2,1)S(1)}, bf16[32,64,128]{2,1,0:T(8,128)(2,1)}, u32[]{:S(2)}) %copy-start) | copy-done | bytes 524312
  1.7 0.0 copy-start.3
  1.7 0.8 %copy-done.3 = bf16[128,128]{1,0:T(8,128)(2,1)S(1)} copy-done((bf16[128,128]{1,0:T(8,128)(2,1)S(1)}, bf16[128,128]{1,0:T(8,128)(2,1)}, u32[]{:S(2)}) %copy-start.3) | copy-done | bytes 32792
  2.5 0.0 copy-start.4
  2.5 0.8 %copy-done.4 = bf16[128,128]{1,0:T(8,128)(2,1)S(1)} copy-done((bf16[128,128]{1,0:T(8,128)(2,1)S(1)}, bf16[128,128]{1,0:T(8,128)(2,1)}, u32[]{:S(2)}) %copy-start.4) | copy-done | bytes 32792
  3.2 0.0 copy-start.5
  3.2 0.8 %copy-done.5 = bf16[128,128]{1,0:T(8,128)(2,1)S(1)} copy-done((bf16[128,128]{1,0:T(8,128)(2,1)S(1)}, bf16[128,128]{1,0:T(8,128)(2,1)}, u32[]{:S(2)}) %copy-start.5) | copy-done | bytes 32792
  4.0 0.0 copy-start.6
  4.0 0.8 %copy-done.6 = bf16[128,128]{1,0:T(8,128)(2,1)S(1)} copy-done((bf16[128,128]{1,0:T(8,128)(2,1)S(1)}, bf16[128,128]{1,0:T(8,128)(2,1)}, u32[]{:S(2)}) %copy-start.6) | copy-done | bytes 32792
  4.7 5.9 %shard_map.109 = bf16[128,32,128]{2,1,0:T(8,128)(2,1)S(1)} custom-call(bf16[32,64,128]{2,1,0:T(8,128)(2,1)S(1)} %copy-done, f32[1,128]{1,0:T(1,128)S(1)} %bitcast.7, f32[1,128]{1,0:T(1,128)S(1)} %bitcast.9, bf16[128,128]{1,0:T(8,128)(2,1)S(1)} %copy-done.3, bf16[128,128]{1,0:T(8,128)(2,1)S(1)} %copy-done.4, bf16[128,128]{1,0:T(8,128)(2,1)S(1)} %copy-done.5, ...), custom_call_target="tpu_custom_call" | custom-call | flops 268435456 | bytes 1048576 | tf_op jit(solution)/shard_map/pallas_call | solution.py:125
  10.6 30.0 %all_to_all.10 = bf16[128,32,128]{2,1,0:T(8,128)(2,1)S(1)} all-to-all(bf16[128,32,128]{2,1,0:T(8,128)(2,1)S(1)} %shard_map.109), channel_id=1, replica_groups=mesh['row'=16,'col'=8] {'row','col'}, dimensions={0} | all-to-all | bytes 2097152 | tf_op jit(solution)/shard_map/all_to_all | solution.py:131
  40.6 1.5 %shard_map.110 = bf16[16,8,16,128]{3,2,1,0:T(8,128)(2,1)} custom-call(bf16[16,8,32,128]{3,2,1,0:T(8,128)(2,1)S(1)} %bitcast.6), custom_call_target="tpu_custom_call" | custom-call | flops 268435456 | bytes 1048576 | tf_op jit(solution)/shard_map/pallas_call | solution.py:136
  42.1 0.0 copy-start.1
  42.1 0.0 copy-start.7
  42.1 4.8 %all-to-all-start.1 = ((bf16[128,16,128]{2,1,0:T(8,128)(2,1)}), bf16[128,16,128]{2,1,0:T(8,128)(2,1)S(1)}, u32[]{:S(2)}, u32[]{:S(2)}) async-start(bf16[128,16,128]{2,1,0:T(8,128)(2,1)} %bitcast.3), calls=%async_computation.1 | async-start | bytes 1048576 | tf_op jit(solution)/shard_map/all_to_all | solution.py:142
  46.9 0.0 copy-done.1
  46.9 0.0 copy-done.7
  46.9 0.0 copy-start.2
  46.9 0.8 %shard_map.111.gate_ref = f32[32,64,128]{2,1,0:T(8,128)S(1)} custom-call(bf16[32,64,128]{2,1,0:T(8,128)(2,1)S(1)} %copy-done.1, f32[1,128]{1,0:T(1,128)S(1)} %bitcast.8, f32[1,128]{1,0:T(1,128)S(1)} %bitcast.10, bf16[128,128]{1,0:T(8,128)(2,1)S(1)} %copy-done.7), custom_call_target="tpu_custom_call" | custom-call | flops 67108864 | bytes 1048576 | tf_op jit(solution)/shard_map/pallas_call | solution.py:132
  47.7 12.6 %all-to-all-done.1.in_ref = bf16[128,16,128]{2,1,0:T(8,128)(2,1)S(1)} async-done(((bf16[128,16,128]{2,1,0:T(8,128)(2,1)}), bf16[128,16,128]{2,1,0:T(8,128)(2,1)S(1)}, u32[]{:S(2)}, u32[]{:S(2)}) %all-to-all-start.1) | async-done | bytes 524320 | tf_op jit(solution)/shard_map/all_to_all | solution.py:142
  60.3 0.0 copy-start.10
  60.4 0.0 copy-start.11
  60.4 0.0 copy-done.2
  60.4 0.6 %copy-done.10 = f32[128]{0:T(128)S(1)} copy-done((f32[128]{0:T(128)S(1)}, f32[128]{0:T(128)}, u32[]{:S(2)}) %copy-start.10) | copy-done | bytes 536
  61.0 0.0 copy-done.11
  61.0 1.7 %shard_map.112 = bf16[32,64,128]{2,1,0:T(8,128)(2,1)} custom-call(bf16[128,16,128]{2,1,0:T(8,128)(2,1)S(1)} %all-to-all-done.1.in_ref, f32[32,64,128]{2,1,0:T(8,128)S(1)} %shard_map.111.gate_ref, f32[1,128]{1,0:T(1,128)S(1)} %bitcast.11, f32[1,128]{1,0:T(1,128)S(1)} %bitcast.12, bf16[128,128]{1,0:T(8,128)(2,1)S(1)} %copy-done.2), custom_call_target="tpu_custom_call" | custom-call | flops 67108864 | bytes 1048576 | tf_op jit(solution)/shard_map/pallas_call | solution.py:143
Async XLA Ops:
  0.0 0.7 %copy-start.8 = (f32[128]{0:T(128)S(1)}, f32[128]{0:T(128)}, u32[]{:S(2)}) copy-start(f32[128]{0:T(128)} %param.12) | copy-start | bytes 1540
  0.0 0.7 %copy-start.9 = (f32[128]{0:T(128)S(1)}, f32[128]{0:T(128)}, u32[]{:S(2)}) copy-start(f32[128]{0:T(128)} %param.13) | copy-start | bytes 1540
  0.7 1.0 %copy-start = (bf16[32,64,128]{2,1,0:T(8,128)(2,1)S(1)}, bf16[32,64,128]{2,1,0:T(8,128)(2,1)}, u32[]{:S(2)}) copy-start(bf16[32,64,128]{2,1,0:T(8,128)(2,1)} %pair_ref.3) | copy-start | bytes 1572868
  1.7 0.8 %copy-start.3 = (bf16[128,128]{1,0:T(8,128)(2,1)S(1)}, bf16[128,128]{1,0:T(8,128)(2,1)}, u32[]{:S(2)}) copy-start(bf16[128,128]{1,0:T(8,128)(2,1)} %ag_ref.1) | copy-start | bytes 98308
  2.5 0.8 %copy-start.4 = (bf16[128,128]{1,0:T(8,128)(2,1)S(1)}, bf16[128,128]{1,0:T(8,128)(2,1)}, u32[]{:S(2)}) copy-start(bf16[128,128]{1,0:T(8,128)(2,1)} %ap_ref.1) | copy-start | bytes 98308
  3.2 0.8 %copy-start.5 = (bf16[128,128]{1,0:T(8,128)(2,1)S(1)}, bf16[128,128]{1,0:T(8,128)(2,1)}, u32[]{:S(2)}) copy-start(bf16[128,128]{1,0:T(8,128)(2,1)} %bg_ref.1) | copy-start | bytes 98308
  4.0 0.8 %copy-start.6 = (bf16[128,128]{1,0:T(8,128)(2,1)S(1)}, bf16[128,128]{1,0:T(8,128)(2,1)}, u32[]{:S(2)}) copy-start(bf16[128,128]{1,0:T(8,128)(2,1)} %bp_ref.1) | copy-start | bytes 98308
  42.1 4.8 %copy-start.1 = (bf16[32,64,128]{2,1,0:T(8,128)(2,1)S(1)}, bf16[32,64,128]{2,1,0:T(8,128)(2,1)}, u32[]{:S(2)}) copy-start(bf16[32,64,128]{2,1,0:T(8,128)(2,1)} %pair_ref.3) | copy-start | bytes 1572868
  42.1 4.8 %copy-start.7 = (bf16[128,128]{1,0:T(8,128)(2,1)S(1)}, bf16[128,128]{1,0:T(8,128)(2,1)}, u32[]{:S(2)}) copy-start(bf16[128,128]{1,0:T(8,128)(2,1)} %weight_ref.2) | copy-start | bytes 98308
  42.1 18.2 %all-to-all-start.1 = ((bf16[128,16,128]{2,1,0:T(8,128)(2,1)}), bf16[128,16,128]{2,1,0:T(8,128)(2,1)S(1)}, u32[]{:S(2)}, u32[]{:S(2)}) async-start(bf16[128,16,128]{2,1,0:T(8,128)(2,1)} %bitcast.3), calls=%async_computation.1 | async-start | bytes 1048576 | tf_op jit(solution)/shard_map/all_to_all | solution.py:142
  46.9 13.5 %copy-start.2 = (bf16[128,128]{1,0:T(8,128)(2,1)S(1)}, bf16[128,128]{1,0:T(8,128)(2,1)}, u32[]{:S(2)}) copy-start(bf16[128,128]{1,0:T(8,128)(2,1)} %weight_ref.3) | copy-start | bytes 98308
  60.3 0.7 %copy-start.10 = (f32[128]{0:T(128)S(1)}, f32[128]{0:T(128)}, u32[]{:S(2)}) copy-start(f32[128]{0:T(128)} %param.19) | copy-start | bytes 1540
  60.4 0.7 %copy-start.11 = (f32[128]{0:T(128)S(1)}, f32[128]{0:T(128)}, u32[]{:S(2)}) copy-start(f32[128]{0:T(128)} %param.20) | copy-start | bytes 1540

commit v2 on v1

--- a/solution.py
+++ b/solution.py
@@ -36,27 +36,70 @@
     return centered * lax.rsqrt(variance + EPS)
 
 
-def operands_kernel(pair_ref, gain_ref, bias_ref, ag_ref, ap_ref, bg_ref, bp_ref, out_ref, wide_ref):
-    rows, cols, chans = pair_ref.shape
+def start(copies):
+    for copy in copies:
+        copy.start()
+    return copies
+
+
+def wait(copies):
+    for copy in copies:
+        copy.wait()
+
+
+def operands_kernel(
+    pair_hbm, gain_hbm, bias_hbm, ag_hbm, ap_hbm, bg_hbm, bp_hbm, out_ref, pair_ref, vector_ref, weight_ref, wide_ref, sem
+):
+    rows, _, chans = pair_hbm.shape
     half = rows // 2
-    tiles = 2 * half
+    small = [pltpu.make_async_copy(ref, weight_ref.at[n], sem.at[n]) for n, ref in enumerate((ag_hbm, ap_hbm, bg_hbm, bp_hbm))]
+    small += [pltpu.make_async_copy(ref, vector_ref.at[pl.ds(n, 1)], sem.at[4 + n]) for n, ref in enumerate((gain_hbm, bias_hbm))]
+    start(small)
+    step = half // PARTS
+    parts = []
+    for n in range(PARTS):
+        spans = [pl.ds(h * half + n * step, step) for h in range(2)]
+        parts.append(
+            start([pltpu.make_async_copy(pair_hbm.at[at], pair_ref.at[at], sem.at[6 + 2 * n + h]) for h, at in enumerate(spans)])
+        )
     eye = identity(chans)
-    gain, bias = column(gain_ref[...], 2 * cols), column(bias_ref[...], 2 * cols)
-    weights = [ref[...].T for ref in (ag_ref, ap_ref, bg_ref, bp_ref)]
-    for s in range(half):
-        block = jnp.concatenate([pair_ref[s], pair_ref[half + s]], axis=0)
-        turned = dot(eye, block, (1, 1))
-        normed = (norm(turned, 0) * gain + bias).astype(BF16)
-        a_gate, a_proj, b_gate, b_proj = (dot(w, normed, (1, 0)) for w in weights)
-        wide_ref[pl.ds(s, chans, stride=tiles), :] = sigmoid(a_gate) * a_proj
-        wide_ref[pl.ds(half + s, chans, stride=tiles), :] = sigmoid(b_gate) * b_proj
-    out_ref[...] = wide_ref[...].astype(BF16).reshape(out_ref.shape)
-
-
-def gate_kernel(pair_ref, gain_ref, bias_ref, weight_ref, out_ref):
-    rows, cols, chans = pair_ref.shape
+    wait(small)
+    weights = jnp.concatenate([weight_ref[n].T for n in range(4)], axis=0)
+    gain, bias = (jnp.concatenate([column(vector_ref[n : n + 1], LANES)] * 2, axis=1) for n in range(2))
+    pitch = 2 * half + 1
+    for s in range(0, half, 2):
+        if s % step == 0:
+            wait(parts[s // step])
+        block = jnp.concatenate([pair_ref[row] for row in (s, half + s, s + 1, half + s + 1)], axis=0)
+        normed = (norm(dot(eye, block, (1, 1)), 0) * gain + bias).astype(BF16)
+        projected = dot(weights, normed, (1, 0))
+        a_gate, a_proj, b_gate, b_proj = (projected[n * chans : (n + 1) * chans] for n in range(4))
+        left, right = sigmoid(a_gate) * a_proj, sigmoid(b_gate) * b_proj
+        for n in range(2):
+            cut = slice(n * LANES, (n + 1) * LANES)
+            wide_ref[pl.ds(s + n, chans, stride=pitch), :] = left[:, cut]
+            wide_ref[pl.ds(half + s + n, chans, stride=pitch), :] = right[:, cut]
+    for c in range(chans):
+        out_ref[c] = wide_ref[pl.ds(c * pitch, 2 * half), :].astype(BF16)
+
+
+def gate_kernel(
+    pair_hbm, gain_hbm, bias_hbm, weight_hbm, mid_gain_hbm, mid_bias_hbm, out_proj_hbm,
+    out_ref, mid_gain_ref, mid_bias_ref, out_proj_ref, pair_ref, vector_ref, weight_ref, sem,
+):
+    rows, cols, chans = pair_hbm.shape
+    copies = [
+        pltpu.make_async_copy(pair_hbm, pair_ref, sem.at[0]),
+        pltpu.make_async_copy(weight_hbm, weight_ref, sem.at[1]),
+        pltpu.make_async_copy(out_proj_hbm, out_proj_ref, sem.at[2]),
+    ]
+    vectors = (gain_hbm, bias_hbm, mid_gain_hbm, mid_bias_hbm)
+    copies += [pltpu.make_async_copy(ref, vector_ref.at[pl.ds(n, 1)], sem.at[3 + n]) for n, ref in enumerate(vectors)]
+    wait(start(copies))
+    mid_gain_ref[...] = column(vector_ref[2:3], LANES)
+    mid_bias_ref[...] = column(vector_ref[3:4], LANES)
     values = pair_ref[...].reshape(rows * cols, chans).astype(F32)
-    normed = (norm(values, 1) * gain_ref[...] + bias_ref[...]).astype(BF16)
+    normed = (norm(values, 1) * vector_ref[0:1] + vector_ref[1:2]).astype(BF16)
     out_ref[...] = sigmoid(dot(normed, weight_ref[...], (1, 0))).reshape(out_ref.shape)
 
 
@@ -89,28 +132,44 @@
             )
 
 
-def update_kernel(in_ref, gate_ref, gain_ref, bias_ref, weight_ref, out_ref, wide_ref):
+def update_kernel(in_ref, gate_ref, gain_ref, bias_ref, weight_ref, out_hbm, wide_ref, out_ref, sem):
     chans, half, lanes = in_ref.shape
     cols = lanes // 2
-    gain, bias = column(gain_ref[...], lanes), column(bias_ref[...], lanes)
-    wide_ref[...] = norm(in_ref[...].astype(F32), 0).reshape(wide_ref.shape)
+    pitch = half + 1
+    normed = norm(in_ref[...].astype(F32), 0)
+    for c in range(chans):
+        wide_ref[pl.ds(c * pitch, half), :] = normed[c]
+    step = half // PARTS
+    copies = []
     for s in range(half):
-        mixed = (wide_ref[pl.ds(s, chans, stride=half), :] * gain + bias).astype(BF16)
+        mixed = (wide_ref[pl.ds(s, chans, stride=pitch), :] * gain_ref[...] + bias_ref[...]).astype(BF16)
         output = dot(mixed, weight_ref[...], (0, 0))
         out_ref[s] = (gate_ref[s] * output[:cols]).astype(BF16)
         out_ref[half + s] = (gate_ref[half + s] * output[cols:]).astype(BF16)
-
-
+        if s % step == step - 1:
+            for h in range(2):
+                at = pl.ds(h * half + s - step + 1, step)
+                copies += start([pltpu.make_async_copy(out_ref.at[at], out_hbm.at[at], sem.at[len(copies)])])
+    wait(copies)
+
+
+LANES = 128
+PARTS = 4
 VMEM_LIMIT = 48 * 2**20
 
 
-def call(kernel, out, scratch=(), flops=0):
+def in_hbm(*arrays):
+    return [pltpu.with_memory_space_constraint(array, pltpu.HBM) for array in arrays]
+
+
+def call(kernel, out, scratch=(), flops=0, **specs):
     return pl.pallas_call(
         kernel,
         out_shape=out,
         scratch_shapes=list(scratch),
         compiler_params=pltpu.CompilerParams(vmem_limit_bytes=VMEM_LIMIT),
         cost_estimate=pl.CostEstimate(flops=flops, bytes_accessed=2**20, transcendentals=2**18),
+        **specs,
     )
 
 
@@ -121,17 +180,39 @@
     hidden = a_gate.shape[1]
     row_count, col_count = lax.axis_size("row"), lax.axis_size("col")
     half, lanes = rows // 2, 2 * cols
+    hbm = pl.BlockSpec(memory_space=pltpu.HBM)
     gain, bias = in_gain[None, :], in_bias[None, :]
     operands = call(
         operands_kernel,
         jax.ShapeDtypeStruct((hidden, 2 * half, lanes), BF16),
-        [pltpu.VMEM((hidden * 2 * half, lanes), F32)],
+        [
+            pltpu.VMEM(pair.shape, BF16),
+            pltpu.VMEM((8, chans), F32),
+            pltpu.VMEM((4, chans, hidden), BF16),
+            pltpu.VMEM(((hidden + 8) * (2 * half + 1), lanes), F32),
+            pltpu.SemaphoreType.DMA((6 + 2 * PARTS,)),
+        ],
         2 * rows * cols * chans * 4 * hidden,
-    )(pair, gain, bias, a_gate, a_proj, b_gate, b_proj)
+        in_specs=[hbm] * 7,
+    )(*in_hbm(pair, gain, bias, a_gate, a_proj, b_gate, b_proj))
     channel = lax.all_to_all(operands, BOTH, 0, 0, tiled=True)
-    gate = call(gate_kernel, jax.ShapeDtypeStruct(pair.shape, F32), (), 2 * rows * cols * chans * chans)(
-        pair, gain, bias, out_gate
-    )
+    gate, mid_gain, mid_bias, out_proj = call(
+        gate_kernel,
+        (
+            jax.ShapeDtypeStruct(pair.shape, F32),
+            jax.ShapeDtypeStruct((hidden, lanes), F32),
+            jax.ShapeDtypeStruct((hidden, lanes), F32),
+            jax.ShapeDtypeStruct(out_proj.shape, BF16),
+        ),
+        [
+            pltpu.VMEM(pair.shape, BF16),
+            pltpu.VMEM((8, chans), F32),
+            pltpu.VMEM(out_gate.shape, BF16),
+            pltpu.SemaphoreType.DMA((7,)),
+        ],
+        2 * rows * cols * chans * chans,
+        in_specs=[hbm] * 7,
+    )(*in_hbm(pair, gain, bias, out_gate, mid_gain[None, :], mid_bias[None, :], out_proj))
     count, depth = row_count * half, col_count * cols
     triangle = call(
         product_kernel,
@@ -139,13 +220,18 @@
         [pltpu.VMEM((row_count, 2, half, depth), BF16), pltpu.VMEM((row_count, 2, half, depth), BF16)],
         8 * count * count * depth,
     )(channel.reshape(row_count, col_count, 2 * half, lanes))
-    triangle = lax.all_to_all(triangle.reshape(operands.shape[0], half, lanes), BOTH, 0, 0, tiled=True)
+    triangle = lax.all_to_all(triangle.reshape(hidden, half, lanes), BOTH, 0, 0, tiled=True)
     return call(
         update_kernel,
         jax.ShapeDtypeStruct(pair.shape, BF16),
-        [pltpu.VMEM((hidden * half, lanes), F32)],
+        [
+            pltpu.VMEM(((hidden + 8) * (half + 1), lanes), F32),
+            pltpu.VMEM(pair.shape, BF16),
+            pltpu.SemaphoreType.DMA((2 * PARTS,)),
+        ],
         2 * rows * cols * hidden * chans,
-    )(triangle, gate, mid_gain[None, :], mid_bias[None, :], out_proj)
+        out_specs=hbm,
+    )(triangle, gate, mid_gain, mid_bias, out_proj)
 
 
 def solution(mesh):

time: 63.5 us -> 54.9 us (0.86)
  local copies, waits for them, and re-layouts: 5.42 us -> 0 us
  Pallas kernels: 9.96 us -> 8.36 us
  waiting for transfers between devices: 12.6 us -> 11.5 us
    unnamed x24 -> x0, local copies, waits for them, and re-layouts: 5.42 us -> none
    pallas_call x1, Pallas kernels: 5.89 us -> 3.35 us  [per_device(): call(operands_kernel, jax.ShapeDtypeStruct((hidden, 2 * half, lanes), BF1...]
    pallas_call x1, Pallas kernels: 0.82 us -> 1.99 us  [per_device(): call(gate_kernel, (jax.ShapeDtypeStruct(pair.shape, F32), jax.ShapeDtypeS...]
    all_to_all x1, waiting for transfers between devices: 12.6 us -> 11.5 us  [per_device(): lax.all_to_all(triangle.reshape(hidden, half, lanes), BOTH, 0, 0, tiled=T...]
  transfers between devices with their start and end apart: 1 -> 1, of which waited for: 1 -> 1; matrix products, arithmetic and copies ran while one was open for 0% -> 0% of each run, Pallas kernels for 1% -> 4%
where the time goes in v2:
time: 54.9 us; the launch traced here: 54.4 us
  blocking collectives  29.9 us (54%)
  waiting for transfers between devices  11.5 us (21%)
  Pallas kernels  8.36 us (15%)
  starting transfers between devices  4.62 us (8%)
    all_to_all x1, blocking collectives, per_device(): channel = lax.all_to_all(operands, BOTH, 0, 0, tiled=True)  29.9 us
    all_to_all x1, waiting for transfers between devices, per_device(): lax.all_to_all(triangle.reshape(hidden, half, lanes), BOTH, 0, 0, tiled=T...  11.5 us
    all_to_all x1, starting transfers between devices, per_device(): lax.all_to_all(triangle.reshape(hidden, half, lanes), BOTH, 0, 0, tiled=T...  4.62 us
    pallas_call x1, Pallas kernels, per_device(): call(operands_kernel, jax.ShapeDtypeStruct((hidden, 2 * half, lanes), BF1...  3.35 us
    pallas_call x1, Pallas kernels, per_device(): call(gate_kernel, (jax.ShapeDtypeStruct(pair.shape, F32), jax.ShapeDtypeS...  1.99 us
    pallas_call x1, Pallas kernels, per_device(): call(product_kernel, jax.ShapeDtypeStruct((row_count, col_count, half, la...  1.52 us
    pallas_call x1, Pallas kernels, per_device(): call(update_kernel, jax.ShapeDtypeStruct(pair.shape, BF16), [pltpu.VMEM((...  1.5 us
  transfers between devices with their start and end apart: 1, of which 1 were waited for; matrix products, arithmetic and copies ran while one was open for 0% of the time, Pallas kernels for 4%

profile of v2, /device:TPU:0, one launch (start us, length us, event | category | flops | bytes accessed | tf_op | source)
XLA Modules:
  0.0 54.4 jit_solution(10019811771640762313)
XLA Ops:
  0.0 3.3 %shard_map.109 = bf16[128,32,128]{2,1,0:T(8,128)(2,1)S(1)} custom-call(bf16[32,64,128]{2,1,0:T(8,128)(2,1)} %pair_hbm.3, f32[1,128]{1,0:T(1,128)} %bitcast.7, f32[1,128]{1,0:T(1,128)} %bitcast.9, bf16[128,128]{1,0:T(8,128)(2,1)} %ag_hbm.1, bf16[128,128]{1,0:T(8,128)(2,1)} %ap_hbm.1, bf16[128,128]{1,0:T(8,128)(2,1)} %bg_hbm.1, bf16[128,128]{1,0:T(8,128)(2,1)} %bp_hbm.1), custom_call_target="tpu_custom_call" | custom-call | flops 268435456 | bytes 1048576 | tf_op jit(solution)/shard_map/pallas_call | solution.py:185
  3.4 29.9 %all_to_all.10 = bf16[128,32,128]{2,1,0:T(8,128)(2,1)S(1)} all-to-all(bf16[128,32,128]{2,1,0:T(8,128)(2,1)S(1)} %shard_map.109), channel_id=1, replica_groups=mesh['row'=16,'col'=8] {'row','col'}, dimensions={0} | all-to-all | bytes 2097152 | tf_op jit(solution)/shard_map/all_to_all | solution.py:198
  33.3 1.5 %shard_map.110 = bf16[16,8,16,128]{3,2,1,0:T(8,128)(2,1)} custom-call(bf16[16,8,32,128]{3,2,1,0:T(8,128)(2,1)S(1)} %bitcast.6), custom_call_target="tpu_custom_call" | custom-call | flops 268435456 | bytes 1048576 | tf_op jit(solution)/shard_map/pallas_call | solution.py:217
  34.8 4.6 %all-to-all-start.1 = ((bf16[128,16,128]{2,1,0:T(8,128)(2,1)}), bf16[128,16,128]{2,1,0:T(8,128)(2,1)S(1)}, u32[]{:S(2)}, u32[]{:S(2)}) async-start(bf16[128,16,128]{2,1,0:T(8,128)(2,1)} %bitcast.3), calls=%async_computation.1 | async-start | bytes 1048576 | tf_op jit(solution)/shard_map/all_to_all | solution.py:223
  39.5 2.0 %shard_map.111 = (f32[32,64,128]{2,1,0:T(8,128)S(1)}, f32[128,128]{1,0:T(8,128)S(1)}, f32[128,128]{1,0:T(8,128)S(1)}, bf16[128,128]{1,0:T(8,128)(2,1)S(1)}) custom-call(bf16[32,64,128]{2,1,0:T(8,128)(2,1)} %pair_hbm.3, f32[1,128]{1,0:T(1,128)} %bitcast.8, f32[1,128]{1,0:T(1,128)} %bitcast.10, bf16[128,128]{1,0:T(8,128)(2,1)} %weight_hbm.1, ...), custom_call_target="tpu_custom_call" | custom-call | flops 67108864 | bytes 1048576 | tf_op jit(solution)/shard_map/pallas_call | solution.py:199
  41.5 11.5 %all-to-all-done.1.in_ref = bf16[128,16,128]{2,1,0:T(8,128)(2,1)S(1)} async-done(((bf16[128,16,128]{2,1,0:T(8,128)(2,1)}), bf16[128,16,128]{2,1,0:T(8,128)(2,1)S(1)}, u32[]{:S(2)}, u32[]{:S(2)}) %all-to-all-start.1) | async-done | bytes 524320 | tf_op jit(solution)/shard_map/all_to_all | solution.py:223
  52.9 1.5 %shard_map.112 = bf16[32,64,128]{2,1,0:T(8,128)(2,1)} custom-call(bf16[128,16,128]{2,1,0:T(8,128)(2,1)S(1)} %all-to-all-done.1.in_ref, f32[32,64,128]{2,1,0:T(8,128)S(1)} %get-tuple-element.9.gate_ref, f32[128,128]{1,0:T(8,128)S(1)} %get-tuple-element.10.gain_ref, f32[128,128]{1,0:T(8,128)S(1)} %get-tuple-element.11.bias_ref, ...), custom_call_target="tpu_custom_call" | custom-call | flops 67108864 | bytes 1048576 | tf_op jit(solution)/shard_map/pallas_call | solution.py:224
Async XLA Ops:
  34.8 18.1 %all-to-all-start.1 = ((bf16[128,16,128]{2,1,0:T(8,128)(2,1)}), bf16[128,16,128]{2,1,0:T(8,128)(2,1)S(1)}, u32[]{:S(2)}, u32[]{:S(2)}) async-start(bf16[128,16,128]{2,1,0:T(8,128)(2,1)} %bitcast.3), calls=%async_computation.1 | async-start | bytes 1048576 | tf_op jit(solution)/shard_map/all_to_all | solution.py:223

commit v3 on v2

--- a/solution.py
+++ b/solution.py
@@ -14,11 +14,9 @@
     return 0.5 + 0.5 * jnp.tanh(0.5 * x)
 
 
-def identity(size):
-    return (
-        lax.broadcasted_iota(jnp.int32, (size, size), 0)
-        == lax.broadcasted_iota(jnp.int32, (size, size), 1)
-    ).astype(BF16)
+def centring(size):
+    same = lax.broadcasted_iota(jnp.int32, (size, size), 0) == lax.broadcasted_iota(jnp.int32, (size, size), 1)
+    return jnp.where(same, 1 - 1 / size, -1 / size).astype(BF16)
 
 
 def dot(a, b, contract):
@@ -55,30 +53,24 @@
     small = [pltpu.make_async_copy(ref, weight_ref.at[n], sem.at[n]) for n, ref in enumerate((ag_hbm, ap_hbm, bg_hbm, bp_hbm))]
     small += [pltpu.make_async_copy(ref, vector_ref.at[pl.ds(n, 1)], sem.at[4 + n]) for n, ref in enumerate((gain_hbm, bias_hbm))]
     start(small)
-    step = half // PARTS
-    parts = []
-    for n in range(PARTS):
-        spans = [pl.ds(h * half + n * step, step) for h in range(2)]
-        parts.append(
-            start([pltpu.make_async_copy(pair_hbm.at[at], pair_ref.at[at], sem.at[6 + 2 * n + h]) for h, at in enumerate(spans)])
-        )
-    eye = identity(chans)
+    fetch = pltpu.make_async_copy(pair_hbm, pair_ref, sem.at[6])
+    fetch.start()
     wait(small)
-    weights = jnp.concatenate([weight_ref[n].T for n in range(4)], axis=0)
-    gain, bias = (jnp.concatenate([column(vector_ref[n : n + 1], LANES)] * 2, axis=1) for n in range(2))
+    weights = jnp.concatenate([weight_ref[n].T * jnp.asarray(0.5, BF16) for n in range(4)], axis=0)
+    gain, bias = (jnp.concatenate([column(vector_ref[n : n + 1], LANES)] * half, axis=1) for n in range(2))
+    fetch.wait()
+    block = jnp.concatenate([pair_ref[row] for s in range(half) for row in (s, half + s)], axis=0)
+    centered = dot(centring(chans), block, (1, 1))
+    variance = jnp.mean(centered * centered, axis=0, keepdims=True)
+    normed = (centered * lax.rsqrt(variance + EPS) * gain + bias).astype(BF16)
+    projected = dot(weights, normed, (1, 0))
+    a_gate, a_proj, b_gate, b_proj = (projected[n * chans : (n + 1) * chans] for n in range(4))
+    left, right = a_proj + jnp.tanh(a_gate) * a_proj, b_proj + jnp.tanh(b_gate) * b_proj
     pitch = 2 * half + 1
-    for s in range(0, half, 2):
-        if s % step == 0:
-            wait(parts[s // step])
-        block = jnp.concatenate([pair_ref[row] for row in (s, half + s, s + 1, half + s + 1)], axis=0)
-        normed = (norm(dot(eye, block, (1, 1)), 0) * gain + bias).astype(BF16)
-        projected = dot(weights, normed, (1, 0))
-        a_gate, a_proj, b_gate, b_proj = (projected[n * chans : (n + 1) * chans] for n in range(4))
-        left, right = sigmoid(a_gate) * a_proj, sigmoid(b_gate) * b_proj
-        for n in range(2):
-            cut = slice(n * LANES, (n + 1) * LANES)
-            wide_ref[pl.ds(s + n, chans, stride=pitch), :] = left[:, cut]
-            wide_ref[pl.ds(half + s + n, chans, stride=pitch), :] = right[:, cut]
+    for s in range(half):
+        cut = slice(s * LANES, (s + 1) * LANES)
+        wide_ref[pl.ds(s, chans, stride=pitch), :] = left[:, cut]
+        wide_ref[pl.ds(half + s, chans, stride=pitch), :] = right[:, cut]
     for c in range(chans):
         out_ref[c] = wide_ref[pl.ds(c * pitch, 2 * half), :].astype(BF16)
 
@@ -103,33 +95,29 @@
     out_ref[...] = sigmoid(dot(normed, weight_ref[...], (1, 0))).reshape(out_ref.shape)
 
 
-def product_kernel(in_ref, out_ref, left_ref, right_ref):
-    row_count, col_count, lanes = in_ref.shape[0], in_ref.shape[1], in_ref.shape[3]
-    tile = in_ref.shape[2] // 2
-    cols = lanes // 2
-    groups = row_count * tile
-    for m in range(col_count // 2):
-        for which, ref in ((0, left_ref), (1, right_ref)):
-            part = pl.ds(which * tile, tile)
-            even = in_ref[:, 2 * m, part, :]
-            odd = in_ref[:, 2 * m + 1, part, :]
-            for h in range(2):
-                ref[:, h, :, m * lanes : (m + 1) * lanes] = jnp.concatenate(
-                    [even[:, :, h * cols : (h + 1) * cols], odd[:, :, h * cols : (h + 1) * cols]], axis=2
-                )
-    depth = right_ref.shape[3]
-    right = right_ref[...].reshape(2 * groups, depth)
-    products = [
-        dot(left_ref[:, h].reshape(groups, depth), right, (1, 1)).astype(BF16).reshape(row_count, tile, 2 * groups)
-        for h in range(2)
-    ]
-    for m in range(col_count // 2):
-        first, second = (p[:, :, m * lanes : (m + 1) * lanes] for p in products)
-        for odd in range(2):
-            cut = slice(odd * cols, (odd + 1) * cols)
-            out_ref[:, 2 * m + odd] = jnp.concatenate(
-                [first[:, :, cut], second[:, :, cut]], axis=2
-            )
+def merge(even, odd, cols):
+    return [jnp.concatenate([even[:, cut], odd[:, cut]], axis=1) for cut in (slice(0, cols), slice(cols, 2 * cols))]
+
+
+def product_kernel(in_ref, out_ref):
+    row_count, col_count, tiles, lanes = in_ref.shape
+    tile, cols, depth = tiles // 2, lanes // 2, col_count * lanes // 2
+    count = row_count * tile
+    pairs = range(col_count // 2)
+
+    def operand(part):
+        parts = [
+            merge(*(in_ref[:, 2 * m + odd, part, :].reshape(count, lanes) for odd in range(2)), cols) for m in pairs
+        ]
+        return [jnp.concatenate([part[h] for part in parts], axis=1) for h in range(2)]
+
+    left, right = operand(pl.ds(0, tile)), operand(pl.ds(tile, tile))
+    right = jnp.stack([half.reshape(row_count, tile, depth) for half in right], axis=1).reshape(2 * count, depth)
+    products = [dot(half, right, (1, 1)).astype(BF16) for half in left]
+    for m in pairs:
+        cut = slice(m * lanes, (m + 1) * lanes)
+        for odd, block in enumerate(merge(*(half[:, cut] for half in products), cols)):
+            out_ref[:, 2 * m + odd] = block.reshape(row_count, tile, lanes)
 
 
 def update_kernel(in_ref, gate_ref, gain_ref, bias_ref, weight_ref, out_hbm, wide_ref, out_ref, sem):
@@ -190,7 +178,7 @@
             pltpu.VMEM((8, chans), F32),
             pltpu.VMEM((4, chans, hidden), BF16),
             pltpu.VMEM(((hidden + 8) * (2 * half + 1), lanes), F32),
-            pltpu.SemaphoreType.DMA((6 + 2 * PARTS,)),
+            pltpu.SemaphoreType.DMA((7,)),
         ],
         2 * rows * cols * chans * 4 * hidden,
         in_specs=[hbm] * 7,
@@ -217,7 +205,7 @@
     triangle = call(
         product_kernel,
         jax.ShapeDtypeStruct((row_count, col_count, half, lanes), BF16),
-        [pltpu.VMEM((row_count, 2, half, depth), BF16), pltpu.VMEM((row_count, 2, half, depth), BF16)],
+        (),
         8 * count * count * depth,
     )(channel.reshape(row_count, col_count, 2 * half, lanes))
     triangle = lax.all_to_all(triangle.reshape(hidden, half, lanes), BOTH, 0, 0, tiled=True)

time: 54.9 us -> 53.7 us (0.978)
  Pallas kernels: 8.36 us -> 7.18 us
    pallas_call x1, Pallas kernels: 3.35 us -> 2.24 us  [per_device(): call(operands_kernel, jax.ShapeDtypeStruct((hidden, 2 * half, lanes), BF1...]
where the time goes in v3:
time: 53.7 us; the launch traced here: 53.2 us
  blocking collectives  29.9 us (56%)
  waiting for transfers between devices  11.5 us (21%)
  Pallas kernels  7.18 us (13%)
  starting transfers between devices  4.62 us (9%)
    all_to_all x1, blocking collectives, per_device(): channel = lax.all_to_all(operands, BOTH, 0, 0, tiled=True)  29.9 us
    all_to_all x1, waiting for transfers between devices, per_device(): lax.all_to_all(triangle.reshape(hidden, half, lanes), BOTH, 0, 0, tiled=T...  11.5 us
    all_to_all x1, starting transfers between devices, per_device(): lax.all_to_all(triangle.reshape(hidden, half, lanes), BOTH, 0, 0, tiled=T...  4.62 us
    pallas_call x1, Pallas kernels, per_device(): call(operands_kernel, jax.ShapeDtypeStruct((hidden, 2 * half, lanes), BF1...  2.24 us
    pallas_call x1, Pallas kernels, per_device(): call(gate_kernel, (jax.ShapeDtypeStruct(pair.shape, F32), jax.ShapeDtypeS...  1.99 us
    pallas_call x1, Pallas kernels, per_device(): call(update_kernel, jax.ShapeDtypeStruct(pair.shape, BF16), [pltpu.VMEM((...  1.5 us
    pallas_call x1, Pallas kernels, per_device(): call(product_kernel, jax.ShapeDtypeStruct((row_count, col_count, half, la...  1.45 us
  transfers between devices with their start and end apart: 1, of which 1 were waited for; matrix products, arithmetic and copies ran while one was open for 0% of the time, Pallas kernels for 4%

profile of v3, /device:TPU:0, one launch (start us, length us, event | category | flops | bytes accessed | tf_op | source)
XLA Modules:
  0.0 53.2 jit_solution(14563146852710550975)
XLA Ops:
  0.0 2.2 %shard_map.109 = bf16[128,32,128]{2,1,0:T(8,128)(2,1)S(1)} custom-call(bf16[32,64,128]{2,1,0:T(8,128)(2,1)} %pair_hbm.3, f32[1,128]{1,0:T(1,128)} %bitcast.7, f32[1,128]{1,0:T(1,128)} %bitcast.9, bf16[128,128]{1,0:T(8,128)(2,1)} %ag_hbm.1, bf16[128,128]{1,0:T(8,128)(2,1)} %ap_hbm.1, bf16[128,128]{1,0:T(8,128)(2,1)} %bg_hbm.1, bf16[128,128]{1,0:T(8,128)(2,1)} %bp_hbm.1), custom_call_target="tpu_custom_call" | custom-call | flops 268435456 | bytes 1048576 | tf_op jit(solution)/shard_map/pallas_call | solution.py:173
  2.2 29.9 %all_to_all.10 = bf16[128,32,128]{2,1,0:T(8,128)(2,1)S(1)} all-to-all(bf16[128,32,128]{2,1,0:T(8,128)(2,1)S(1)} %shard_map.109), channel_id=1, replica_groups=mesh['row'=16,'col'=8] {'row','col'}, dimensions={0} | all-to-all | bytes 2097152 | tf_op jit(solution)/shard_map/all_to_all | solution.py:186
  32.2 1.4 %shard_map.110 = bf16[16,8,16,128]{3,2,1,0:T(8,128)(2,1)} custom-call(bf16[16,8,32,128]{3,2,1,0:T(8,128)(2,1)S(1)} %bitcast.6), custom_call_target="tpu_custom_call" | custom-call | flops 268435456 | bytes 1048576 | tf_op jit(solution)/shard_map/pallas_call | solution.py:205
  33.6 4.6 %all-to-all-start.1 = ((bf16[128,16,128]{2,1,0:T(8,128)(2,1)}), bf16[128,16,128]{2,1,0:T(8,128)(2,1)S(1)}, u32[]{:S(2)}, u32[]{:S(2)}) async-start(bf16[128,16,128]{2,1,0:T(8,128)(2,1)} %bitcast.3), calls=%async_computation.1 | async-start | bytes 1048576 | tf_op jit(solution)/shard_map/all_to_all | solution.py:211
  38.3 2.0 %shard_map.111 = (f32[32,64,128]{2,1,0:T(8,128)S(1)}, f32[128,128]{1,0:T(8,128)S(1)}, f32[128,128]{1,0:T(8,128)S(1)}, bf16[128,128]{1,0:T(8,128)(2,1)S(1)}) custom-call(bf16[32,64,128]{2,1,0:T(8,128)(2,1)} %pair_hbm.3, f32[1,128]{1,0:T(1,128)} %bitcast.8, f32[1,128]{1,0:T(1,128)} %bitcast.10, bf16[128,128]{1,0:T(8,128)(2,1)} %weight_hbm.1, ...), custom_call_target="tpu_custom_call" | custom-call | flops 67108864 | bytes 1048576 | tf_op jit(solution)/shard_map/pallas_call | solution.py:187
  40.3 11.5 %all-to-all-done.1.in_ref = bf16[128,16,128]{2,1,0:T(8,128)(2,1)S(1)} async-done(((bf16[128,16,128]{2,1,0:T(8,128)(2,1)}), bf16[128,16,128]{2,1,0:T(8,128)(2,1)S(1)}, u32[]{:S(2)}, u32[]{:S(2)}) %all-to-all-start.1) | async-done | bytes 524320 | tf_op jit(solution)/shard_map/all_to_all | solution.py:211
  51.7 1.5 %shard_map.112 = bf16[32,64,128]{2,1,0:T(8,128)(2,1)} custom-call(bf16[128,16,128]{2,1,0:T(8,128)(2,1)S(1)} %all-to-all-done.1.in_ref, f32[32,64,128]{2,1,0:T(8,128)S(1)} %get-tuple-element.9.gate_ref, f32[128,128]{1,0:T(8,128)S(1)} %get-tuple-element.10.gain_ref, f32[128,128]{1,0:T(8,128)S(1)} %get-tuple-element.11.bias_ref, ...), custom_call_target="tpu_custom_call" | custom-call | flops 67108864 | bytes 1048576 | tf_op jit(solution)/shard_map/pallas_call | solution.py:212
Async XLA Ops:
  33.6 18.1 %all-to-all-start.1 = ((bf16[128,16,128]{2,1,0:T(8,128)(2,1)}), bf16[128,16,128]{2,1,0:T(8,128)(2,1)S(1)}, u32[]{:S(2)}, u32[]{:S(2)}) async-start(bf16[128,16,128]{2,1,0:T(8,128)(2,1)} %bitcast.3), calls=%async_computation.1 | async-start | bytes 1048576 | tf_op jit(solution)/shard_map/all_to_all | solution.py:211

commit v4 on v3

--- a/solution.py
+++ b/solution.py
@@ -46,23 +46,31 @@
 
 
 def operands_kernel(
-    pair_hbm, gain_hbm, bias_hbm, ag_hbm, ap_hbm, bg_hbm, bp_hbm, out_ref, pair_ref, vector_ref, weight_ref, wide_ref, sem
+    pair_hbm, gain_hbm, bias_hbm, ag_hbm, ap_hbm, bg_hbm, bp_hbm, gate_hbm, mid_gain_hbm, mid_bias_hbm, proj_hbm,
+    out_ref, normed_ref, mid_gain_ref, mid_bias_ref, late_ref, pair_ref, vector_ref, weight_ref, wide_ref, sem,
 ):
     rows, _, chans = pair_hbm.shape
     half = rows // 2
-    small = [pltpu.make_async_copy(ref, weight_ref.at[n], sem.at[n]) for n, ref in enumerate((ag_hbm, ap_hbm, bg_hbm, bp_hbm))]
-    small += [pltpu.make_async_copy(ref, vector_ref.at[pl.ds(n, 1)], sem.at[4 + n]) for n, ref in enumerate((gain_hbm, bias_hbm))]
+    weights = (ag_hbm, ap_hbm, bg_hbm, bp_hbm, gate_hbm, proj_hbm)
+    vectors = (gain_hbm, bias_hbm, mid_gain_hbm, mid_bias_hbm)
+    small = [pltpu.make_async_copy(ref, weight_ref.at[n], sem.at[n]) for n, ref in enumerate(weights)]
+    small += [
+        pltpu.make_async_copy(ref, vector_ref.at[pl.ds(n, 1)], sem.at[len(weights) + n]) for n, ref in enumerate(vectors)
+    ]
     start(small)
-    fetch = pltpu.make_async_copy(pair_hbm, pair_ref, sem.at[6])
+    fetch = pltpu.make_async_copy(pair_hbm, pair_ref, sem.at[len(small)])
     fetch.start()
     wait(small)
     weights = jnp.concatenate([weight_ref[n].T * jnp.asarray(0.5, BF16) for n in range(4)], axis=0)
     gain, bias = (jnp.concatenate([column(vector_ref[n : n + 1], LANES)] * half, axis=1) for n in range(2))
+    mid_gain_ref[...], mid_bias_ref[...] = (column(vector_ref[n : n + 1], LANES) for n in (2, 3))
+    late_ref[...] = weight_ref[pl.ds(4, 2)] * jnp.asarray(0.5, BF16)
     fetch.wait()
     block = jnp.concatenate([pair_ref[row] for s in range(half) for row in (s, half + s)], axis=0)
     centered = dot(centring(chans), block, (1, 1))
     variance = jnp.mean(centered * centered, axis=0, keepdims=True)
     normed = (centered * lax.rsqrt(variance + EPS) * gain + bias).astype(BF16)
+    normed_ref[...] = normed
     projected = dot(weights, normed, (1, 0))
     a_gate, a_proj, b_gate, b_proj = (projected[n * chans : (n + 1) * chans] for n in range(4))
     left, right = a_proj + jnp.tanh(a_gate) * a_proj, b_proj + jnp.tanh(b_gate) * b_proj
@@ -75,26 +83,6 @@
         out_ref[c] = wide_ref[pl.ds(c * pitch, 2 * half), :].astype(BF16)
 
 
-def gate_kernel(
-    pair_hbm, gain_hbm, bias_hbm, weight_hbm, mid_gain_hbm, mid_bias_hbm, out_proj_hbm,
-    out_ref, mid_gain_ref, mid_bias_ref, out_proj_ref, pair_ref, vector_ref, weight_ref, sem,
-):
-    rows, cols, chans = pair_hbm.shape
-    copies = [
-        pltpu.make_async_copy(pair_hbm, pair_ref, sem.at[0]),
-        pltpu.make_async_copy(weight_hbm, weight_ref, sem.at[1]),
-        pltpu.make_async_copy(out_proj_hbm, out_proj_ref, sem.at[2]),
-    ]
-    vectors = (gain_hbm, bias_hbm, mid_gain_hbm, mid_bias_hbm)
-    copies += [pltpu.make_async_copy(ref, vector_ref.at[pl.ds(n, 1)], sem.at[3 + n]) for n, ref in enumerate(vectors)]
-    wait(start(copies))
-    mid_gain_ref[...] = column(vector_ref[2:3], LANES)
-    mid_bias_ref[...] = column(vector_ref[3:4], LANES)
-    values = pair_ref[...].reshape(rows * cols, chans).astype(F32)
-    normed = (norm(values, 1) * vector_ref[0:1] + vector_ref[1:2]).astype(BF16)
-    out_ref[...] = sigmoid(dot(normed, weight_ref[...], (1, 0))).reshape(out_ref.shape)
-
-
 def merge(even, odd, cols):
     return [jnp.concatenate([even[:, cut], odd[:, cut]], axis=1) for cut in (slice(0, cols), slice(cols, 2 * cols))]
 
@@ -113,14 +101,15 @@
 
     left, right = operand(pl.ds(0, tile)), operand(pl.ds(tile, tile))
     right = jnp.stack([half.reshape(row_count, tile, depth) for half in right], axis=1).reshape(2 * count, depth)
-    products = [dot(half, right, (1, 1)).astype(BF16) for half in left]
+    product = dot(jnp.concatenate(left, axis=0), right, (1, 1)).astype(BF16)
+    products = [product[:count], product[count:]]
     for m in pairs:
         cut = slice(m * lanes, (m + 1) * lanes)
         for odd, block in enumerate(merge(*(half[:, cut] for half in products), cols)):
             out_ref[:, 2 * m + odd] = block.reshape(row_count, tile, lanes)
 
 
-def update_kernel(in_ref, gate_ref, gain_ref, bias_ref, weight_ref, out_hbm, wide_ref, out_ref, sem):
+def update_kernel(in_ref, normed_ref, gain_ref, bias_ref, weight_ref, out_hbm, wide_ref, out_ref, sem):
     chans, half, lanes = in_ref.shape
     cols = lanes // 2
     pitch = half + 1
@@ -131,9 +120,10 @@
     copies = []
     for s in range(half):
         mixed = (wide_ref[pl.ds(s, chans, stride=pitch), :] * gain_ref[...] + bias_ref[...]).astype(BF16)
-        output = dot(mixed, weight_ref[...], (0, 0))
-        out_ref[s] = (gate_ref[s] * output[:cols]).astype(BF16)
-        out_ref[half + s] = (gate_ref[half + s] * output[cols:]).astype(BF16)
+        output = dot(mixed, weight_ref[1], (0, 0))
+        gate = jnp.tanh(dot(normed_ref[:, s * lanes : (s + 1) * lanes], weight_ref[0], (0, 0)))
+        update = (output + gate * output).astype(BF16)
+        out_ref[s], out_ref[half + s] = update[:cols], update[cols:]
         if s % step == step - 1:
             for h in range(2):
                 at = pl.ds(h * half + s - step + 1, step)
@@ -169,38 +159,32 @@
     row_count, col_count = lax.axis_size("row"), lax.axis_size("col")
     half, lanes = rows // 2, 2 * cols
     hbm = pl.BlockSpec(memory_space=pltpu.HBM)
-    gain, bias = in_gain[None, :], in_bias[None, :]
-    operands = call(
+    late = jax.ShapeDtypeStruct((hidden, lanes), F32)
+    operands, normed, mid_gain, mid_bias, weights = call(
         operands_kernel,
-        jax.ShapeDtypeStruct((hidden, 2 * half, lanes), BF16),
-        [
-            pltpu.VMEM(pair.shape, BF16),
-            pltpu.VMEM((8, chans), F32),
-            pltpu.VMEM((4, chans, hidden), BF16),
-            pltpu.VMEM(((hidden + 8) * (2 * half + 1), lanes), F32),
-            pltpu.SemaphoreType.DMA((7,)),
-        ],
-        2 * rows * cols * chans * 4 * hidden,
-        in_specs=[hbm] * 7,
-    )(*in_hbm(pair, gain, bias, a_gate, a_proj, b_gate, b_proj))
-    channel = lax.all_to_all(operands, BOTH, 0, 0, tiled=True)
-    gate, mid_gain, mid_bias, out_proj = call(
-        gate_kernel,
         (
-            jax.ShapeDtypeStruct(pair.shape, F32),
-            jax.ShapeDtypeStruct((hidden, lanes), F32),
-            jax.ShapeDtypeStruct((hidden, lanes), F32),
-            jax.ShapeDtypeStruct(out_proj.shape, BF16),
+            jax.ShapeDtypeStruct((hidden, 2 * half, lanes), BF16),
+            jax.ShapeDtypeStruct((chans, rows * cols), BF16),
+            late,
+            late,
+            jax.ShapeDtypeStruct((2, chans, hidden), BF16),
         ),
         [
             pltpu.VMEM(pair.shape, BF16),
             pltpu.VMEM((8, chans), F32),
-            pltpu.VMEM(out_gate.shape, BF16),
-            pltpu.SemaphoreType.DMA((7,)),
+            pltpu.VMEM((6, chans, hidden), BF16),
+            pltpu.VMEM(((hidden + 8) * (2 * half + 1), lanes), F32),
+            pltpu.SemaphoreType.DMA((11,)),
         ],
-        2 * rows * cols * chans * chans,
-        in_specs=[hbm] * 7,
-    )(*in_hbm(pair, gain, bias, out_gate, mid_gain[None, :], mid_bias[None, :], out_proj))
+        2 * rows * cols * chans * 4 * hidden,
+        in_specs=[hbm] * 11,
+    )(
+        *in_hbm(
+            pair, in_gain[None, :], in_bias[None, :], a_gate, a_proj, b_gate, b_proj,
+            out_gate, mid_gain[None, :], mid_bias[None, :], out_proj,
+        )
+    )
+    channel = lax.all_to_all(operands, BOTH, 0, 0, tiled=True)
     count, depth = row_count * half, col_count * cols
     triangle = call(
         product_kernel,
@@ -219,7 +203,7 @@
         ],
         2 * rows * cols * hidden * chans,
         out_specs=hbm,
-    )(triangle, gate, mid_gain, mid_bias, out_proj)
+    )(triangle, normed, mid_gain, mid_bias, weights)
 
 
 def solution(mesh):

time: 53.7 us -> 52.5 us (0.978)
  blocking collectives: 29.9 us -> 47.5 us
  waiting for transfers between devices: 11.5 us -> 0 us
  starting transfers between devices: 4.62 us -> 0 us
  Pallas kernels: 7.18 us -> 4.57 us
    all_to_all x0 -> x1, blocking collectives: none -> 17.6 us  [per_device(): lax.all_to_all(triangle.reshape(hidden, half, lanes), BOTH, 0, 0, tiled=T...]
    all_to_all x1 -> x0, waiting for transfers between devices: 11.5 us -> none  [per_device(): lax.all_to_all(triangle.reshape(hidden, half, lanes), BOTH, 0, 0, tiled=T...]
    all_to_all x1 -> x0, starting transfers between devices: 4.62 us -> none  [per_device(): lax.all_to_all(triangle.reshape(hidden, half, lanes), BOTH, 0, 0, tiled=T...]
    pallas_call x2 -> x1, Pallas kernels: 4.23 us -> 2.33 us  [per_device(): call(operands_kernel, (jax.ShapeDtypeStruct((hidden, 2 * half, lanes), BF...]
    pallas_call x1, Pallas kernels: 1.45 us -> 0.62 us  [per_device(): call(product_kernel, jax.ShapeDtypeStruct((row_count, col_count, half, la...]
  transfers between devices with their start and end apart: 1 -> 0, of which waited for: 1 -> 0; matrix products, arithmetic and copies ran while one was open for 0% -> 0% of each run, Pallas kernels for 4% -> 0%
where the time goes in v4:
time: 52.5 us; the launch traced here: 52.1 us
  blocking collectives  47.5 us (90%)
  Pallas kernels  4.57 us (9%)
    all_to_all x1, blocking collectives, per_device(): channel = lax.all_to_all(operands, BOTH, 0, 0, tiled=True)  29.9 us
    all_to_all x1, blocking collectives, per_device(): lax.all_to_all(triangle.reshape(hidden, half, lanes), BOTH, 0, 0, tiled=T...  17.6 us
    pallas_call x1, Pallas kernels, per_device(): call(operands_kernel, (jax.ShapeDtypeStruct((hidden, 2 * half, lanes), BF...  2.33 us
    pallas_call x1, Pallas kernels, per_device(): call(update_kernel, jax.ShapeDtypeStruct(pair.shape, BF16), [pltpu.VMEM((...  1.61 us

profile of v4, /device:TPU:0, one launch (start us, length us, event | category | flops | bytes accessed | tf_op | source)
XLA Modules:
  0.0 52.1 jit_solution(13999593751071254557)
XLA Ops:
  0.0 2.3 %shard_map.109 = (bf16[128,32,128]{2,1,0:T(8,128)(2,1)S(1)}, bf16[128,2048]{1,0:T(8,128)(2,1)S(1)}, f32[128,128]{1,0:T(8,128)S(1)}, f32[128,128]{1,0:T(8,128)S(1)}, bf16[2,128,128]{2,1,0:T(8,128)(2,1)S(1)}) custom-call(bf16[32,64,128]{2,1,0:T(8,128)(2,1)} %pair_hbm.1, f32[1,128]{1,0:T(1,128)} %bitcast.8, f32[1,128]{1,0:T(1,128)} %bitcast.9, ...), custom_call_target="tpu_custom_call" | custom-call | flops 268435456 | bytes 1048576 | tf_op jit(solution)/shard_map/pallas_call | solution.py:163
  2.3 29.9 %all_to_all.10 = bf16[128,32,128]{2,1,0:T(8,128)(2,1)S(1)} all-to-all(bf16[128,32,128]{2,1,0:T(8,128)(2,1)S(1)} %get-tuple-element.10), channel_id=1, replica_groups=mesh['row'=16,'col'=8] {'row','col'}, dimensions={0} | all-to-all | bytes 2097152 | tf_op jit(solution)/shard_map/all_to_all | solution.py:187
  32.3 0.6 %shard_map.110 = bf16[16,8,16,128]{3,2,1,0:T(8,128)(2,1)S(1)} custom-call(bf16[16,8,32,128]{3,2,1,0:T(8,128)(2,1)S(1)} %bitcast.6), custom_call_target="tpu_custom_call" | custom-call | flops 268435456 | bytes 1048576 | tf_op jit(solution)/shard_map/pallas_call | solution.py:189
  32.9 17.6 %all_to_all.11.in_ref = bf16[128,16,128]{2,1,0:T(8,128)(2,1)S(1)} all-to-all(bf16[128,16,128]{2,1,0:T(8,128)(2,1)S(1)} %bitcast.7), channel_id=1, replica_groups=mesh['row'=16,'col'=8] {'row','col'}, dimensions={0} | all-to-all | bytes 1048576 | tf_op jit(solution)/shard_map/all_to_all | solution.py:195
  50.5 1.6 %shard_map.111 = bf16[32,64,128]{2,1,0:T(8,128)(2,1)} custom-call(bf16[128,16,128]{2,1,0:T(8,128)(2,1)S(1)} %all_to_all.11.in_ref, bf16[128,2048]{1,0:T(8,128)(2,1)S(1)} %get-tuple-element.11.normed_ref, f32[128,128]{1,0:T(8,128)S(1)} %get-tuple-element.12.gain_ref, f32[128,128]{1,0:T(8,128)S(1)} %get-tuple-element.13.bias_ref, ...), custom_call_target="tpu_custom_call" | custom-call | flops 67108864 | bytes 1048576 | tf_op jit(solution)/shard_map/pallas_call | solution.py:196

commit v5 on v4

--- a/solution.py
+++ b/solution.py
@@ -1,3 +1,5 @@
+import functools
+
 import jax
 import jax.numpy as jnp
 from jax import lax
@@ -8,6 +10,20 @@
 BF16, F32 = jnp.bfloat16, jnp.float32
 EPS = 1e-05
 BOTH = ("row", "col")
+FIRST = (6, 2)
+
+
+def chips(row_count, col_count):
+    first = FIRST[0] * col_count + FIRST[1]
+    return [first] + [n for n in range(row_count // 2 * col_count) if n != first]
+
+
+def exchange(values, row_count, col_count):
+    devices = [
+        [(2 * (n // col_count) + core) * col_count + n % col_count for n in chips(row_count, col_count)]
+        for core in range(2)
+    ]
+    return lax.all_to_all(values, BOTH, 0, 0, axis_index_groups=devices, tiled=True)
 
 
 def sigmoid(x):
@@ -87,26 +103,35 @@
     return [jnp.concatenate([even[:, cut], odd[:, cut]], axis=1) for cut in (slice(0, cols), slice(cols, 2 * cols))]
 
 
-def product_kernel(in_ref, out_ref):
-    row_count, col_count, tiles, lanes = in_ref.shape
-    tile, cols, depth = tiles // 2, lanes // 2, col_count * lanes // 2
-    count = row_count * tile
-    pairs = range(col_count // 2)
-
-    def operand(part):
-        parts = [
-            merge(*(in_ref[:, 2 * m + odd, part, :].reshape(count, lanes) for odd in range(2)), cols) for m in pairs
-        ]
-        return [jnp.concatenate([part[h] for part in parts], axis=1) for h in range(2)]
-
-    left, right = operand(pl.ds(0, tile)), operand(pl.ds(tile, tile))
-    right = jnp.stack([half.reshape(row_count, tile, depth) for half in right], axis=1).reshape(2 * count, depth)
-    product = dot(jnp.concatenate(left, axis=0), right, (1, 1)).astype(BF16)
-    products = [product[:count], product[count:]]
-    for m in pairs:
-        cut = slice(m * lanes, (m + 1) * lanes)
-        for odd, block in enumerate(merge(*(half[:, cut] for half in products), cols)):
-            out_ref[:, 2 * m + odd] = block.reshape(row_count, tile, lanes)
+def arrange_kernel(order, part, in_ref, out_ref):
+    channels, rows, _, tile, depth = out_ref.shape
+    lanes = in_ref.shape[3]
+    count = 2 * depth // lanes
+    for channel in range(channels):
+        for row in range(rows):
+            tiles = [in_ref[order.index(row * count + col), channel, pl.ds(part * tile, tile), :] for col in range(count)]
+            for m in range(count // 2):
+                for h, block in enumerate(merge(tiles[2 * m], tiles[2 * m + 1], lanes // 2)):
+                    out_ref[channel, row, h, :, m * lanes : (m + 1) * lanes] = block
+
+
+def product_kernel(order, left_ref, right_ref, other_ref, out_ref):
+    channels, rows, _, tile, depth = left_ref.shape
+    lanes = out_ref.shape[3]
+    cols, count = lanes // 2, rows * tile
+    core = lax.rem(lax.axis_index("row"), 2)
+    for channel in range(channels):
+        own, other = right_ref[channel], other_ref[channel]
+        right = jnp.stack([jnp.where(core == 0, own, other), jnp.where(core == 0, other, own)], axis=1)
+        right = right.reshape(4 * count, depth)
+        left = jnp.concatenate([left_ref[channel, :, h].reshape(count, depth) for h in range(2)], axis=0)
+        product = dot(left, right, (1, 1)).astype(BF16)
+        for m in range(4 * count // lanes):
+            cut = slice(m * lanes, (m + 1) * lanes)
+            for odd, block in enumerate(merge(product[:count, cut], product[count:, cut], cols)):
+                for row in range(rows):
+                    at = order.index(row * (4 * count // cols) + 2 * m + odd)
+                    out_ref[at, channel] = block[row * tile : (row + 1) * tile]
 
 
 def update_kernel(in_ref, normed_ref, gain_ref, bias_ref, weight_ref, out_hbm, wide_ref, out_ref, sem):
@@ -184,15 +209,23 @@
             out_gate, mid_gain[None, :], mid_bias[None, :], out_proj,
         )
     )
-    channel = lax.all_to_all(operands, BOTH, 0, 0, tiled=True)
-    count, depth = row_count * half, col_count * cols
+    order = chips(row_count, col_count)
+    count, depth = row_count // 2, col_count * cols
+    messages = exchange(operands.reshape(len(order), 4 * half, lanes), row_count, col_count)
+    messages = messages.reshape(len(order), 2, 2 * half, lanes)
+    arranged = jax.ShapeDtypeStruct((2, count, 2, half, depth), BF16)
+    left, right = (
+        call(functools.partial(arrange_kernel, order, part), arranged)(messages) for part in range(2)
+    )
+    other = lax.ppermute(right, "row", [(row, row ^ 1) for row in range(row_count)])
     triangle = call(
-        product_kernel,
-        jax.ShapeDtypeStruct((row_count, col_count, half, lanes), BF16),
+        functools.partial(product_kernel, order),
+        jax.ShapeDtypeStruct((len(order), 2, half, lanes), BF16),
         (),
-        8 * count * count * depth,
-    )(channel.reshape(row_count, col_count, 2 * half, lanes))
-    triangle = lax.all_to_all(triangle.reshape(hidden, half, lanes), BOTH, 0, 0, tiled=True)
+        2 * 2 * (2 * count * half) * (4 * count * half) * depth,
+    )(left, right, other)
+    triangle = exchange(triangle.reshape(len(order), 2 * half, lanes), row_count, col_count)
+    triangle = triangle.reshape(hidden, half, lanes)
     return call(
         update_kernel,
         jax.ShapeDtypeStruct(pair.shape, BF16),

time: 52.5 us -> 49.7 us (0.947)
  blocking collectives: 47.5 us -> 42.8 us
  waiting for transfers between devices: 0 us -> 1.69 us
    all_to_all x2, blocking collectives: 47.5 us -> 42.8 us  [exchange(): lax.all_to_all(values, BOTH, 0, 0, axis_index_groups=devices, tiled=True)]
    ppermute x0 -> x1, waiting for transfers between devices: none -> 1.69 us  [per_device(): lax.ppermute(right, 'row', [(row, row ^ 1) for row in range(row_count)])]
  transfers between devices with their start and end apart: 0 -> 1, of which waited for: 0 -> 1; matrix products, arithmetic and copies ran while one was open for 0% -> 0% of each run, Pallas kernels for 0% -> 0%
where the time goes in v5:
time: 49.7 us; the launch traced here: 49.5 us
  blocking collectives  42.8 us (86%)
  Pallas kernels  4.91 us (10%)
  waiting for transfers between devices  1.69 us (3%)
    all_to_all x2, blocking collectives, exchange(): lax.all_to_all(values, BOTH, 0, 0, axis_index_groups=devices, tiled=True)  42.8 us
    pallas_call x1, Pallas kernels, per_device(): call(operands_kernel, (jax.ShapeDtypeStruct((hidden, 2 * half, lanes), BF...  2.33 us
    ppermute x1, waiting for transfers between devices, per_device(): lax.ppermute(right, 'row', [(row, row ^ 1) for row in range(row_count)])  1.69 us
    pallas_call x1, Pallas kernels, per_device(): call(update_kernel, jax.ShapeDtypeStruct(pair.shape, BF16), [pltpu.VMEM((...  1.61 us
  transfers between devices with their start and end apart: 1, of which 1 were waited for; matrix products, arithmetic and copies ran while one was open for 0% of the time, Pallas kernels for 0%

profile of v5, /device:TPU:0, one launch (start us, length us, event | category | flops | bytes accessed | tf_op | source)
XLA Modules:
  0.0 49.5 jit_solution(6130415276585221681)
XLA Ops:
  0.0 2.3 %shard_map.109 = (bf16[128,32,128]{2,1,0:T(8,128)(2,1)S(1)}, bf16[128,2048]{1,0:T(8,128)(2,1)S(1)}, f32[128,128]{1,0:T(8,128)S(1)}, f32[128,128]{1,0:T(8,128)S(1)}, bf16[2,128,128]{2,1,0:T(8,128)(2,1)S(1)}) custom-call(bf16[32,64,128]{2,1,0:T(8,128)(2,1)} %pair_hbm.1, f32[1,128]{1,0:T(1,128)} %bitcast.13, f32[1,128]{1,0:T(1,128)} %bitcast.14, ...), custom_call_target="tpu_custom_call" | custom-call | flops 268435456 | bytes 1048576 | tf_op jit(solution)/shard_map/pallas_call | solution.py:188
  2.3 25.7 %all_to_all.10 = bf16[64,64,128]{2,1,0:T(8,128)(2,1)S(1)} all-to-all(bf16[64,64,128]{2,1,0:T(8,128)(2,1)S(1)} %bitcast.12), channel_id=1, replica_groups={{98,0,1,2,3,4,5,6,7,16,17,18,19,20,21,22,23,32,33,34,35,36,37,38,39,48,..., dimensions={0} | all-to-all | bytes 2097152 | tf_op jit(solution)/shard_map/all_to_all | solution.py:26
  28.0 0.2 shard_map.111.right_ref
  28.2 0.1 collective-permute-start
  28.3 0.2 shard_map.110.left_ref
  28.5 1.7 %collective-permute-done.other_ref = bf16[2,8,2,16,512]{4,3,2,1,0:T(8,128)(2,1)S(1)} collective-permute-done((bf16[2,8,2,16,512]{4,3,2,1,0:T(8,128)(2,1)S(1)}, bf16[2,8,2,16,512]{4,3,2,1,0:T(8,128)(2,1)S(1)}, u32[]{:S(2)}, u32[]{:S(2)}) %collective-permute-start) | collective-permute-done | bytes 524320 | tf_op jit(solution)/shard_map/ppermute | solution.py:220
  30.2 0.6 %shard_map.112 = bf16[64,2,16,128]{3,2,1,0:T(8,128)(2,1)S(1)} custom-call(bf16[2,8,2,16,512]{4,3,2,1,0:T(8,128)(2,1)S(1)} %shard_map.110.left_ref, bf16[2,8,2,16,512]{4,3,2,1,0:T(8,128)(2,1)S(1)} %shard_map.111.right_ref, bf16[2,8,2,16,512]{4,3,2,1,0:T(8,128)(2,1)S(1)} %collective-permute-done.other_ref), custom_call_target="tpu_custom_call" | custom-call | flops 268435456 | bytes 1048576 | tf_op jit(solution)/shard_map/pallas_call | solution.py:221
  30.8 17.2 %all_to_all.11 = bf16[64,32,128]{2,1,0:T(8,128)(2,1)S(1)} all-to-all(bf16[64,32,128]{2,1,0:T(8,128)(2,1)S(1)} %bitcast.11), channel_id=1, replica_groups={{98,0,1,2,3,4,5,6,7,16,17,18,19,20,21,22,23,32,33,34,35,36,37,38,39,48,..., dimensions={0} | all-to-all | bytes 1048576 | tf_op jit(solution)/shard_map/all_to_all | solution.py:26
  47.9 1.6 %shard_map.113 = bf16[32,64,128]{2,1,0:T(8,128)(2,1)} custom-call(bf16[128,16,128]{2,1,0:T(8,128)(2,1)S(1)} %bitcast.10, bf16[128,2048]{1,0:T(8,128)(2,1)S(1)} %get-tuple-element.11.normed_ref, f32[128,128]{1,0:T(8,128)S(1)} %get-tuple-element.12.gain_ref, f32[128,128]{1,0:T(8,128)S(1)} %get-tuple-element.13.bias_ref, ...), custom_call_target="tpu_custom_call" | custom-call | flops 67108864 | bytes 1048576 | tf_op jit(solution)/shard_map/pallas_call | solution.py:229
Async XLA Ops:
  28.2 2.0 %collective-permute-start = (bf16[2,8,2,16,512]{4,3,2,1,0:T(8,128)(2,1)S(1)}, bf16[2,8,2,16,512]{4,3,2,1,0:T(8,128)(2,1)S(1)}, u32[]{:S(2)}, u32[]{:S(2)}) collective-permute-start(bf16[2,8,2,16,512]{4,3,2,1,0:T(8,128)(2,1)S(1)} %shard_map.111.right_ref), channel_id=1, source_target_pairs={{0,8},{8,0},{16,24},{24,16},{32,40},{40,32},{48,56},{56,48},{64,72... | collective-permute-start | bytes 1572872 | tf_op jit(solution)/shard_map/ppermute | solution.py:220

commit v6 on v5

--- a/solution.py
+++ b/solution.py
@@ -73,9 +73,9 @@
     small += [
         pltpu.make_async_copy(ref, vector_ref.at[pl.ds(n, 1)], sem.at[len(weights) + n]) for n, ref in enumerate(vectors)
     ]
-    start(small)
     fetch = pltpu.make_async_copy(pair_hbm, pair_ref, sem.at[len(small)])
     fetch.start()
+    start(small)
     wait(small)
     weights = jnp.concatenate([weight_ref[n].T * jnp.asarray(0.5, BF16) for n in range(4)], axis=0)
     gain, bias = (jnp.concatenate([column(vector_ref[n : n + 1], LANES)] * half, axis=1) for n in range(2))
@@ -115,6 +115,13 @@
                     out_ref[channel, row, h, :, m * lanes : (m + 1) * lanes] = block
 
 
+def gate_kernel(order, in_ref, normed_ref, weight_ref, out_ref, gate_ref):
+    arrange_kernel(order, 0, in_ref, out_ref)
+    half, lanes, _ = gate_ref.shape
+    for s in range(half):
+        gate_ref[s] = 1 + jnp.tanh(dot(normed_ref[:, s * lanes : (s + 1) * lanes], weight_ref[0], (0, 0)))
+
+
 def product_kernel(order, left_ref, right_ref, other_ref, out_ref):
     channels, rows, _, tile, depth = left_ref.shape
     lanes = out_ref.shape[3]
@@ -134,7 +141,7 @@
                     out_ref[at, channel] = block[row * tile : (row + 1) * tile]
 
 
-def update_kernel(in_ref, normed_ref, gain_ref, bias_ref, weight_ref, out_hbm, wide_ref, out_ref, sem):
+def update_kernel(in_ref, gate_ref, gain_ref, bias_ref, weight_ref, out_hbm, wide_ref, out_ref, sem):
     chans, half, lanes = in_ref.shape
     cols = lanes // 2
     pitch = half + 1
@@ -146,8 +153,7 @@
     for s in range(half):
         mixed = (wide_ref[pl.ds(s, chans, stride=pitch), :] * gain_ref[...] + bias_ref[...]).astype(BF16)
         output = dot(mixed, weight_ref[1], (0, 0))
-        gate = jnp.tanh(dot(normed_ref[:, s * lanes : (s + 1) * lanes], weight_ref[0], (0, 0)))
-        update = (output + gate * output).astype(BF16)
+        update = (gate_ref[s] * output).astype(BF16)
         out_ref[s], out_ref[half + s] = update[:cols], update[cols:]
         if s % step == step - 1:
             for h in range(2):
@@ -214,10 +220,11 @@
     messages = exchange(operands.reshape(len(order), 4 * half, lanes), row_count, col_count)
     messages = messages.reshape(len(order), 2, 2 * half, lanes)
     arranged = jax.ShapeDtypeStruct((2, count, 2, half, depth), BF16)
-    left, right = (
-        call(functools.partial(arrange_kernel, order, part), arranged)(messages) for part in range(2)
-    )
+    right = call(functools.partial(arrange_kernel, order, 1), arranged)(messages)
     other = lax.ppermute(right, "row", [(row, row ^ 1) for row in range(row_count)])
+    left, gate = call(
+        functools.partial(gate_kernel, order), (arranged, jax.ShapeDtypeStruct((half, lanes, chans), F32))
+    )(messages, normed, weights)
     triangle = call(
         functools.partial(product_kernel, order),
         jax.ShapeDtypeStruct((len(order), 2, half, lanes), BF16),
@@ -236,7 +243,7 @@
         ],
         2 * rows * cols * hidden * chans,
         out_specs=hbm,
-    )(triangle, normed, mid_gain, mid_bias, weights)
+    )(triangle, gate, mid_gain, mid_bias, weights)
 
 
 def solution(mesh):

time: 49.7 us -> 49.6 us (level)
  transfers between devices with their start and end apart: 1 -> 1, of which waited for: 1 -> 1; matrix products, arithmetic and copies ran while one was open for 0% -> 0% of each run, Pallas kernels for 0% -> 1%
where the time goes in v6:
time: 49.6 us; the launch traced here: 49.4 us
  blocking collectives  42.8 us (86%)
  Pallas kernels  4.96 us (10%)
  waiting for transfers between devices  1.5 us (3%)
    all_to_all x2, blocking collectives, exchange(): lax.all_to_all(values, BOTH, 0, 0, axis_index_groups=devices, tiled=True)  42.8 us
    pallas_call x1, Pallas kernels, per_device(): call(operands_kernel, (jax.ShapeDtypeStruct((hidden, 2 * half, lanes), BF...  2.32 us
    ppermute x1, waiting for transfers between devices, per_device(): lax.ppermute(right, 'row', [(row, row ^ 1) for row in range(row_count)])  1.5 us
    pallas_call x1, Pallas kernels, per_device(): call(update_kernel, jax.ShapeDtypeStruct(pair.shape, BF16), [pltpu.VMEM((...  1.5 us
  transfers between devices with their start and end apart: 1, of which 1 were waited for; matrix products, arithmetic and copies ran while one was open for 0% of the time, Pallas kernels for 1%

profile of v6, /device:TPU:0, one launch (start us, length us, event | category | flops | bytes accessed | tf_op | source)
XLA Modules:
  0.0 49.4 jit_solution(1678516883158735906)
XLA Ops:
  0.0 2.3 %shard_map.109 = (bf16[128,32,128]{2,1,0:T(8,128)(2,1)S(1)}, bf16[128,2048]{1,0:T(8,128)(2,1)S(1)}, f32[128,128]{1,0:T(8,128)S(1)}, f32[128,128]{1,0:T(8,128)S(1)}, bf16[2,128,128]{2,1,0:T(8,128)(2,1)S(1)}) custom-call(bf16[32,64,128]{2,1,0:T(8,128)(2,1)} %pair_hbm.1, f32[1,128]{1,0:T(1,128)} %bitcast.13, f32[1,128]{1,0:T(1,128)} %bitcast.14, ...), custom_call_target="tpu_custom_call" | custom-call | flops 268435456 | bytes 1048576 | tf_op jit(solution)/shard_map/pallas_call | solution.py:194
  2.3 25.6 %all_to_all.10 = bf16[64,64,128]{2,1,0:T(8,128)(2,1)S(1)} all-to-all(bf16[64,64,128]{2,1,0:T(8,128)(2,1)S(1)} %bitcast.12), channel_id=1, replica_groups={{98,0,1,2,3,4,5,6,7,16,17,18,19,20,21,22,23,32,33,34,35,36,37,38,39,48,..., dimensions={0} | all-to-all | bytes 2097152 | tf_op jit(solution)/shard_map/all_to_all | solution.py:26
  28.0 0.2 shard_map.111.right_ref
  28.2 0.1 collective-permute-start
  28.3 0.4 shard_map.110
  28.7 1.5 %collective-permute-done.other_ref = bf16[2,8,2,16,512]{4,3,2,1,0:T(8,128)(2,1)S(1)} collective-permute-done((bf16[2,8,2,16,512]{4,3,2,1,0:T(8,128)(2,1)S(1)}, bf16[2,8,2,16,512]{4,3,2,1,0:T(8,128)(2,1)S(1)}, u32[]{:S(2)}, u32[]{:S(2)}) %collective-permute-start) | collective-permute-done | bytes 524320 | tf_op jit(solution)/shard_map/ppermute | solution.py:224
  30.2 0.6 %shard_map.112 = bf16[64,2,16,128]{3,2,1,0:T(8,128)(2,1)S(1)} custom-call(bf16[2,8,2,16,512]{4,3,2,1,0:T(8,128)(2,1)S(1)} %get-tuple-element.15.left_ref, bf16[2,8,2,16,512]{4,3,2,1,0:T(8,128)(2,1)S(1)} %shard_map.111.right_ref, bf16[2,8,2,16,512]{4,3,2,1,0:T(8,128)(2,1)S(1)} %collective-permute-done.other_ref), custom_call_target="tpu_custom_call" | custom-call | flops 268435456 | bytes 1048576 | tf_op jit(solution)/shard_map/pallas_call | solution.py:228
  30.7 17.2 %all_to_all.11 = bf16[64,32,128]{2,1,0:T(8,128)(2,1)S(1)} all-to-all(bf16[64,32,128]{2,1,0:T(8,128)(2,1)S(1)} %bitcast.11), channel_id=1, replica_groups={{98,0,1,2,3,4,5,6,7,16,17,18,19,20,21,22,23,32,33,34,35,36,37,38,39,48,..., dimensions={0} | all-to-all | bytes 1048576 | tf_op jit(solution)/shard_map/all_to_all | solution.py:26
  47.9 1.5 %shard_map.113 = bf16[32,64,128]{2,1,0:T(8,128)(2,1)} custom-call(bf16[128,16,128]{2,1,0:T(8,128)(2,1)S(1)} %bitcast.10, f32[16,128,128]{2,1,0:T(8,128)S(1)} %get-tuple-element.16.gate_ref, f32[128,128]{1,0:T(8,128)S(1)} %get-tuple-element.17.gain_ref, f32[128,128]{1,0:T(8,128)S(1)} %get-tuple-element.18.bias_ref, ...), custom_call_target="tpu_custom_call" | custom-call | flops 67108864 | bytes 1048576 | tf_op jit(solution)/shard_map/pallas_call | solution.py:236
Async XLA Ops:
  28.2 2.0 %collective-permute-start = (bf16[2,8,2,16,512]{4,3,2,1,0:T(8,128)(2,1)S(1)}, bf16[2,8,2,16,512]{4,3,2,1,0:T(8,128)(2,1)S(1)}, u32[]{:S(2)}, u32[]{:S(2)}) collective-permute-start(bf16[2,8,2,16,512]{4,3,2,1,0:T(8,128)(2,1)S(1)} %shard_map.111.right_ref), channel_id=1, source_target_pairs={{0,8},{8,0},{16,24},{24,16},{32,40},{40,32},{48,56},{56,48},{64,72... | collective-permute-start | bytes 1572872 | tf_op jit(solution)/shard_map/ppermute | solution.py:224

commit v7 on v6

--- a/solution.py
+++ b/solution.py
@@ -62,13 +62,12 @@
 
 
 def operands_kernel(
-    pair_hbm, gain_hbm, bias_hbm, ag_hbm, ap_hbm, bg_hbm, bp_hbm, gate_hbm, mid_gain_hbm, mid_bias_hbm, proj_hbm,
-    out_ref, normed_ref, mid_gain_ref, mid_bias_ref, late_ref, pair_ref, vector_ref, weight_ref, wide_ref, sem,
+    pair_hbm, gain_hbm, bias_hbm, ag_hbm, ap_hbm, bg_hbm, bp_hbm,
+    out_ref, normed_ref, pair_ref, vector_ref, weight_ref, wide_ref, sem,
 ):
     rows, _, chans = pair_hbm.shape
     half = rows // 2
-    weights = (ag_hbm, ap_hbm, bg_hbm, bp_hbm, gate_hbm, proj_hbm)
-    vectors = (gain_hbm, bias_hbm, mid_gain_hbm, mid_bias_hbm)
+    weights, vectors = (ag_hbm, ap_hbm, bg_hbm, bp_hbm), (gain_hbm, bias_hbm)
     small = [pltpu.make_async_copy(ref, weight_ref.at[n], sem.at[n]) for n, ref in enumerate(weights)]
     small += [
         pltpu.make_async_copy(ref, vector_ref.at[pl.ds(n, 1)], sem.at[len(weights) + n]) for n, ref in enumerate(vectors)
@@ -79,8 +78,6 @@
     wait(small)
     weights = jnp.concatenate([weight_ref[n].T * jnp.asarray(0.5, BF16) for n in range(4)], axis=0)
     gain, bias = (jnp.concatenate([column(vector_ref[n : n + 1], LANES)] * half, axis=1) for n in range(2))
-    mid_gain_ref[...], mid_bias_ref[...] = (column(vector_ref[n : n + 1], LANES) for n in (2, 3))
-    late_ref[...] = weight_ref[pl.ds(4, 2)] * jnp.asarray(0.5, BF16)
     fetch.wait()
     block = jnp.concatenate([pair_ref[row] for s in range(half) for row in (s, half + s)], axis=0)
     centered = dot(centring(chans), block, (1, 1))
@@ -115,11 +112,23 @@
                     out_ref[channel, row, h, :, m * lanes : (m + 1) * lanes] = block
 
 
-def gate_kernel(order, in_ref, normed_ref, weight_ref, out_ref, gate_ref):
+def gate_kernel(
+    order, in_ref, normed_ref, gate_hbm, proj_hbm, gain_hbm, bias_hbm,
+    out_ref, gate_ref, gain_ref, bias_ref, proj_ref, vector_ref, weight_ref, sem,
+):
+    copies = [pltpu.make_async_copy(ref, weight_ref.at[n], sem.at[n]) for n, ref in enumerate((gate_hbm, proj_hbm))]
+    copies += [
+        pltpu.make_async_copy(ref, vector_ref.at[pl.ds(n, 1)], sem.at[2 + n]) for n, ref in enumerate((gain_hbm, bias_hbm))
+    ]
+    start(copies)
     arrange_kernel(order, 0, in_ref, out_ref)
+    wait(copies)
+    gain_ref[...], bias_ref[...] = (column(vector_ref[n : n + 1], LANES) for n in range(2))
+    proj_ref[...] = weight_ref[1] * jnp.asarray(0.5, BF16)
+    weight = weight_ref[0] * jnp.asarray(0.5, BF16)
     half, lanes, _ = gate_ref.shape
     for s in range(half):
-        gate_ref[s] = 1 + jnp.tanh(dot(normed_ref[:, s * lanes : (s + 1) * lanes], weight_ref[0], (0, 0)))
+        gate_ref[s] = 1 + jnp.tanh(dot(normed_ref[:, s * lanes : (s + 1) * lanes], weight, (0, 0)))
 
 
 def product_kernel(order, left_ref, right_ref, other_ref, out_ref):
@@ -152,7 +161,7 @@
     copies = []
     for s in range(half):
         mixed = (wide_ref[pl.ds(s, chans, stride=pitch), :] * gain_ref[...] + bias_ref[...]).astype(BF16)
-        output = dot(mixed, weight_ref[1], (0, 0))
+        output = dot(mixed, weight_ref[...], (0, 0))
         update = (gate_ref[s] * output).astype(BF16)
         out_ref[s], out_ref[half + s] = update[:cols], update[cols:]
         if s % step == step - 1:
@@ -190,31 +199,22 @@
     row_count, col_count = lax.axis_size("row"), lax.axis_size("col")
     half, lanes = rows // 2, 2 * cols
     hbm = pl.BlockSpec(memory_space=pltpu.HBM)
-    late = jax.ShapeDtypeStruct((hidden, lanes), F32)
-    operands, normed, mid_gain, mid_bias, weights = call(
+    operands, normed = call(
         operands_kernel,
         (
             jax.ShapeDtypeStruct((hidden, 2 * half, lanes), BF16),
             jax.ShapeDtypeStruct((chans, rows * cols), BF16),
-            late,
-            late,
-            jax.ShapeDtypeStruct((2, chans, hidden), BF16),
         ),
         [
             pltpu.VMEM(pair.shape, BF16),
             pltpu.VMEM((8, chans), F32),
-            pltpu.VMEM((6, chans, hidden), BF16),
+            pltpu.VMEM((4, chans, hidden), BF16),
             pltpu.VMEM(((hidden + 8) * (2 * half + 1), lanes), F32),
-            pltpu.SemaphoreType.DMA((11,)),
+            pltpu.SemaphoreType.DMA((7,)),
         ],
         2 * rows * cols * chans * 4 * hidden,
-        in_specs=[hbm] * 11,
-    )(
-        *in_hbm(
-            pair, in_gain[None, :], in_bias[None, :], a_gate, a_proj, b_gate, b_proj,
-            out_gate, mid_gain[None, :], mid_bias[None, :], out_proj,
-        )
-    )
+        in_specs=[hbm] * 7,
+    )(*in_hbm(pair, in_gain[None, :], in_bias[None, :], a_gate, a_proj, b_gate, b_proj))
     order = chips(row_count, col_count)
     count, depth = row_count // 2, col_count * cols
     messages = exchange(operands.reshape(len(order), 4 * half, lanes), row_count, col_count)
@@ -222,9 +222,23 @@
     arranged = jax.ShapeDtypeStruct((2, count, 2, half, depth), BF16)
     right = call(functools.partial(arrange_kernel, order, 1), arranged)(messages)
     other = lax.ppermute(right, "row", [(row, row ^ 1) for row in range(row_count)])
-    left, gate = call(
-        functools.partial(gate_kernel, order), (arranged, jax.ShapeDtypeStruct((half, lanes, chans), F32))
-    )(messages, normed, weights)
+    late = jax.ShapeDtypeStruct((hidden, lanes), F32)
+    left, gate, mid_gain, mid_bias, out_proj = call(
+        functools.partial(gate_kernel, order),
+        (
+            arranged,
+            jax.ShapeDtypeStruct((half, lanes, chans), F32),
+            late,
+            late,
+            jax.ShapeDtypeStruct(out_proj.shape, BF16),
+        ),
+        [
+            pltpu.VMEM((8, hidden), F32),
+            pltpu.VMEM((2, chans, hidden), BF16),
+            pltpu.SemaphoreType.DMA((4,)),
+        ],
+        in_specs=[pl.BlockSpec()] * 2 + [hbm] * 4,
+    )(messages, normed, *in_hbm(out_gate, out_proj, mid_gain[None, :], mid_bias[None, :]))
     triangle = call(
         functools.partial(product_kernel, order),
         jax.ShapeDtypeStruct((len(order), 2, half, lanes), BF16),
@@ -243,7 +257,7 @@
         ],
         2 * rows * cols * hidden * chans,
         out_specs=hbm,
-    )(triangle, gate, mid_gain, mid_bias, weights)
+    )(triangle, gate, mid_gain, mid_bias, out_proj)
 
 
 def solution(mesh):

time: 49.6 us -> 49.5 us (level)
  waiting for transfers between devices: 1.5 us -> 0.7 us
  Pallas kernels: 4.96 us -> 5.65 us
    ppermute x1, waiting for transfers between devices: 1.5 us -> 0.7 us  [per_device(): lax.ppermute(right, 'row', [(row, row ^ 1) for row in range(row_count)])]
    pallas_call x1, Pallas kernels: 0.39 us -> 1.19 us  [per_device(): call(functools.partial(gate_kernel, order), (arranged, jax.ShapeDtypeStru...]
  transfers between devices with their start and end apart: 1 -> 1, of which waited for: 1 -> 1; matrix products, arithmetic and copies ran while one was open for 0% -> 0% of each run, Pallas kernels for 1% -> 2%
where the time goes in v7:
time: 49.5 us; the launch traced here: 49.3 us
  blocking collectives  42.8 us (86%)
  Pallas kernels  5.65 us (11%)
  waiting for transfers between devices  0.7 us (1%)
    all_to_all x2, blocking collectives, exchange(): lax.all_to_all(values, BOTH, 0, 0, axis_index_groups=devices, tiled=True)  42.8 us
    pallas_call x1, Pallas kernels, per_device(): call(operands_kernel, (jax.ShapeDtypeStruct((hidden, 2 * half, lanes), BF...  2.2 us
    pallas_call x1, Pallas kernels, per_device(): call(update_kernel, jax.ShapeDtypeStruct(pair.shape, BF16), [pltpu.VMEM((...  1.5 us
    pallas_call x1, Pallas kernels, per_device(): call(functools.partial(gate_kernel, order), (arranged, jax.ShapeDtypeStru...  1.19 us
  transfers between devices with their start and end apart: 1, of which 1 were waited for; matrix products, arithmetic and copies ran while one was open for 0% of the time, Pallas kernels for 2%

profile of v7, /device:TPU:0, one launch (start us, length us, event | category | flops | bytes accessed | tf_op | source)
XLA Modules:
  0.0 49.3 jit_solution(9825627226866930587)
XLA Ops:
  0.0 2.2 %shard_map.109 = (bf16[128,32,128]{2,1,0:T(8,128)(2,1)S(1)}, bf16[128,2048]{1,0:T(8,128)(2,1)S(1)}) custom-call(bf16[32,64,128]{2,1,0:T(8,128)(2,1)} %pair_hbm.1, f32[1,128]{1,0:T(1,128)} %bitcast.15, f32[1,128]{1,0:T(1,128)} %bitcast.16, bf16[128,128]{1,0:T(8,128)(2,1)} %ag_hbm.1, bf16[128,128]{1,0:T(8,128)(2,1)} %ap_hbm.1, bf16[128,128]{1,0:T(8,128)(2,1)} %bg_hbm.1, ...), custom_call_target="tpu_custom_call" | custom-call | flops 268435456 | bytes 1048576 | tf_op jit(solution)/shard_map/pallas_call | solution.py:202
  2.2 25.6 %all_to_all.10 = bf16[64,64,128]{2,1,0:T(8,128)(2,1)S(1)} all-to-all(bf16[64,64,128]{2,1,0:T(8,128)(2,1)S(1)} %bitcast.12), channel_id=1, replica_groups={{98,0,1,2,3,4,5,6,7,16,17,18,19,20,21,22,23,32,33,34,35,36,37,38,39,48,..., dimensions={0} | all-to-all | bytes 2097152 | tf_op jit(solution)/shard_map/all_to_all | solution.py:26
  27.8 0.2 shard_map.111.right_ref
  28.0 0.1 collective-permute-start
  28.1 1.2 %shard_map.110 = (bf16[2,8,2,16,512]{4,3,2,1,0:T(8,128)(2,1)S(1)}, f32[16,128,128]{2,1,0:T(8,128)S(1)}, f32[128,128]{1,0:T(8,128)S(1)}, f32[128,128]{1,0:T(8,128)S(1)}, bf16[128,128]{1,0:T(8,128)(2,1)S(1)}) custom-call(bf16[64,2,32,128]{3,2,1,0:T(8,128)(2,1)S(1)} %bitcast.9, bf16[128,2048]{1,0:T(8,128)(2,1)S(1)} %get-tuple-element.13.normed_ref, ...), custom_call_target="tpu_custom_call" | custom-call | bytes 1048576 | tf_op jit(solution)/shard_map/pallas_call | solution.py:226
  29.3 0.7 %collective-permute-done.other_ref = bf16[2,8,2,16,512]{4,3,2,1,0:T(8,128)(2,1)S(1)} collective-permute-done((bf16[2,8,2,16,512]{4,3,2,1,0:T(8,128)(2,1)S(1)}, bf16[2,8,2,16,512]{4,3,2,1,0:T(8,128)(2,1)S(1)}, u32[]{:S(2)}, u32[]{:S(2)}) %collective-permute-start) | collective-permute-done | bytes 524320 | tf_op jit(solution)/shard_map/ppermute | solution.py:224
  30.0 0.6 %shard_map.112 = bf16[64,2,16,128]{3,2,1,0:T(8,128)(2,1)S(1)} custom-call(bf16[2,8,2,16,512]{4,3,2,1,0:T(8,128)(2,1)S(1)} %get-tuple-element.14.left_ref, bf16[2,8,2,16,512]{4,3,2,1,0:T(8,128)(2,1)S(1)} %shard_map.111.right_ref, bf16[2,8,2,16,512]{4,3,2,1,0:T(8,128)(2,1)S(1)} %collective-permute-done.other_ref), custom_call_target="tpu_custom_call" | custom-call | flops 268435456 | bytes 1048576 | tf_op jit(solution)/shard_map/pallas_call | solution.py:242
  30.6 17.2 %all_to_all.11 = bf16[64,32,128]{2,1,0:T(8,128)(2,1)S(1)} all-to-all(bf16[64,32,128]{2,1,0:T(8,128)(2,1)S(1)} %bitcast.11), channel_id=1, replica_groups={{98,0,1,2,3,4,5,6,7,16,17,18,19,20,21,22,23,32,33,34,35,36,37,38,39,48,..., dimensions={0} | all-to-all | bytes 1048576 | tf_op jit(solution)/shard_map/all_to_all | solution.py:26
  47.8 1.5 %shard_map.113 = bf16[32,64,128]{2,1,0:T(8,128)(2,1)} custom-call(bf16[128,16,128]{2,1,0:T(8,128)(2,1)S(1)} %bitcast.10, f32[16,128,128]{2,1,0:T(8,128)S(1)} %get-tuple-element.15.gate_ref, f32[128,128]{1,0:T(8,128)S(1)} %get-tuple-element.16.gain_ref, f32[128,128]{1,0:T(8,128)S(1)} %get-tuple-element.17.bias_ref, ...), custom_call_target="tpu_custom_call" | custom-call | flops 67108864 | bytes 1048576 | tf_op jit(solution)/shard_map/pallas_call | solution.py:250
Async XLA Ops:
  28.0 2.0 %collective-permute-start = (bf16[2,8,2,16,512]{4,3,2,1,0:T(8,128)(2,1)S(1)}, bf16[2,8,2,16,512]{4,3,2,1,0:T(8,128)(2,1)S(1)}, u32[]{:S(2)}, u32[]{:S(2)}) collective-permute-start(bf16[2,8,2,16,512]{4,3,2,1,0:T(8,128)(2,1)S(1)} %shard_map.111.right_ref), channel_id=1, source_target_pairs={{0,8},{8,0},{16,24},{24,16},{32,40},{40,32},{48,56},{56,48},{64,72... | collective-permute-start | bytes 1572872 | tf_op jit(solution)/shard_map/ppermute | solution.py:224

commit v8 on v7

--- a/solution.py
+++ b/solution.py
@@ -24,10 +24,6 @@
         for core in range(2)
     ]
     return lax.all_to_all(values, BOTH, 0, 0, axis_index_groups=devices, tiled=True)
-
-
-def sigmoid(x):
-    return 0.5 + 0.5 * jnp.tanh(0.5 * x)
 
 
 def centring(size):

time: 49.5 us -> 49.5 us (level)
  no operation moved by 1% of the time
where the time goes in v8:
time: 49.5 us; the launch traced here: 49.3 us
  blocking collectives  42.8 us (86%)
  Pallas kernels  5.65 us (11%)
  waiting for transfers between devices  0.7 us (1%)
    all_to_all x2, blocking collectives, exchange(): lax.all_to_all(values, BOTH, 0, 0, axis_index_groups=devices, tiled=True)  42.8 us
    pallas_call x1, Pallas kernels, per_device(): call(operands_kernel, (jax.ShapeDtypeStruct((hidden, 2 * half, lanes), BF...  2.2 us
    pallas_call x1, Pallas kernels, per_device(): call(update_kernel, jax.ShapeDtypeStruct(pair.shape, BF16), [pltpu.VMEM((...  1.5 us
    pallas_call x1, Pallas kernels, per_device(): call(functools.partial(gate_kernel, order), (arranged, jax.ShapeDtypeStru...  1.19 us
  transfers between devices with their start and end apart: 1, of which 1 were waited for; matrix products, arithmetic and copies ran while one was open for 0% of the time, Pallas kernels for 2%

profile of v8, /device:TPU:0, one launch (start us, length us, event | category | flops | bytes accessed | tf_op | source)
XLA Modules:
  0.0 49.3 jit_solution(9825627226866930587)
XLA Ops:
  0.0 2.2 %shard_map.109 = (bf16[128,32,128]{2,1,0:T(8,128)(2,1)S(1)}, bf16[128,2048]{1,0:T(8,128)(2,1)S(1)}) custom-call(bf16[32,64,128]{2,1,0:T(8,128)(2,1)} %pair_hbm.1, f32[1,128]{1,0:T(1,128)} %bitcast.15, f32[1,128]{1,0:T(1,128)} %bitcast.16, bf16[128,128]{1,0:T(8,128)(2,1)} %ag_hbm.1, bf16[128,128]{1,0:T(8,128)(2,1)} %ap_hbm.1, bf16[128,128]{1,0:T(8,128)(2,1)} %bg_hbm.1, ...), custom_call_target="tpu_custom_call" | custom-call | flops 268435456 | bytes 1048576 | tf_op jit(solution)/shard_map/pallas_call | solution.py:198
  2.2 25.6 %all_to_all.10 = bf16[64,64,128]{2,1,0:T(8,128)(2,1)S(1)} all-to-all(bf16[64,64,128]{2,1,0:T(8,128)(2,1)S(1)} %bitcast.12), channel_id=1, replica_groups={{98,0,1,2,3,4,5,6,7,16,17,18,19,20,21,22,23,32,33,34,35,36,37,38,39,48,..., dimensions={0} | all-to-all | bytes 2097152 | tf_op jit(solution)/shard_map/all_to_all | solution.py:26
  27.8 0.2 shard_map.111.right_ref
  28.0 0.1 collective-permute-start
  28.1 1.2 %shard_map.110 = (bf16[2,8,2,16,512]{4,3,2,1,0:T(8,128)(2,1)S(1)}, f32[16,128,128]{2,1,0:T(8,128)S(1)}, f32[128,128]{1,0:T(8,128)S(1)}, f32[128,128]{1,0:T(8,128)S(1)}, bf16[128,128]{1,0:T(8,128)(2,1)S(1)}) custom-call(bf16[64,2,32,128]{3,2,1,0:T(8,128)(2,1)S(1)} %bitcast.9, bf16[128,2048]{1,0:T(8,128)(2,1)S(1)} %get-tuple-element.13.normed_ref, ...), custom_call_target="tpu_custom_call" | custom-call | bytes 1048576 | tf_op jit(solution)/shard_map/pallas_call | solution.py:222
  29.3 0.7 %collective-permute-done.other_ref = bf16[2,8,2,16,512]{4,3,2,1,0:T(8,128)(2,1)S(1)} collective-permute-done((bf16[2,8,2,16,512]{4,3,2,1,0:T(8,128)(2,1)S(1)}, bf16[2,8,2,16,512]{4,3,2,1,0:T(8,128)(2,1)S(1)}, u32[]{:S(2)}, u32[]{:S(2)}) %collective-permute-start) | collective-permute-done | bytes 524320 | tf_op jit(solution)/shard_map/ppermute | solution.py:220
  30.0 0.6 %shard_map.112 = bf16[64,2,16,128]{3,2,1,0:T(8,128)(2,1)S(1)} custom-call(bf16[2,8,2,16,512]{4,3,2,1,0:T(8,128)(2,1)S(1)} %get-tuple-element.14.left_ref, bf16[2,8,2,16,512]{4,3,2,1,0:T(8,128)(2,1)S(1)} %shard_map.111.right_ref, bf16[2,8,2,16,512]{4,3,2,1,0:T(8,128)(2,1)S(1)} %collective-permute-done.other_ref), custom_call_target="tpu_custom_call" | custom-call | flops 268435456 | bytes 1048576 | tf_op jit(solution)/shard_map/pallas_call | solution.py:238
  30.6 17.2 %all_to_all.11 = bf16[64,32,128]{2,1,0:T(8,128)(2,1)S(1)} all-to-all(bf16[64,32,128]{2,1,0:T(8,128)(2,1)S(1)} %bitcast.11), channel_id=1, replica_groups={{98,0,1,2,3,4,5,6,7,16,17,18,19,20,21,22,23,32,33,34,35,36,37,38,39,48,..., dimensions={0} | all-to-all | bytes 1048576 | tf_op jit(solution)/shard_map/all_to_all | solution.py:26
  47.8 1.5 %shard_map.113 = bf16[32,64,128]{2,1,0:T(8,128)(2,1)} custom-call(bf16[128,16,128]{2,1,0:T(8,128)(2,1)S(1)} %bitcast.10, f32[16,128,128]{2,1,0:T(8,128)S(1)} %get-tuple-element.15.gate_ref, f32[128,128]{1,0:T(8,128)S(1)} %get-tuple-element.16.gain_ref, f32[128,128]{1,0:T(8,128)S(1)} %get-tuple-element.17.bias_ref, ...), custom_call_target="tpu_custom_call" | custom-call | flops 67108864 | bytes 1048576 | tf_op jit(solution)/shard_map/pallas_call | solution.py:246
Async XLA Ops:
  28.0 2.0 %collective-permute-start = (bf16[2,8,2,16,512]{4,3,2,1,0:T(8,128)(2,1)S(1)}, bf16[2,8,2,16,512]{4,3,2,1,0:T(8,128)(2,1)S(1)}, u32[]{:S(2)}, u32[]{:S(2)}) collective-permute-start(bf16[2,8,2,16,512]{4,3,2,1,0:T(8,128)(2,1)S(1)} %shard_map.111.right_ref), channel_id=1, source_target_pairs={{0,8},{8,0},{16,24},{24,16},{32,40},{40,32},{48,56},{56,48},{64,72... | collective-permute-start | bytes 1572872 | tf_op jit(solution)/shard_map/ppermute | solution.py:220

commit v9 on v8

--- a/solution.py
+++ b/solution.py
@@ -137,7 +137,7 @@
         right = jnp.stack([jnp.where(core == 0, own, other), jnp.where(core == 0, other, own)], axis=1)
         right = right.reshape(4 * count, depth)
         left = jnp.concatenate([left_ref[channel, :, h].reshape(count, depth) for h in range(2)], axis=0)
-        product = dot(left, right, (1, 1)).astype(BF16)
+        product = dot(left, right, (1, 1))
         for m in range(4 * count // lanes):
             cut = slice(m * lanes, (m + 1) * lanes)
             for odd, block in enumerate(merge(product[:count, cut], product[count:, cut], cols)):
@@ -150,7 +150,7 @@
     chans, half, lanes = in_ref.shape
     cols = lanes // 2
     pitch = half + 1
-    normed = norm(in_ref[...].astype(F32), 0)
+    normed = norm(in_ref[...], 0)
     for c in range(chans):
         wide_ref[pl.ds(c * pitch, half), :] = normed[c]
     step = half // PARTS
@@ -237,7 +237,7 @@
     )(messages, normed, *in_hbm(out_gate, out_proj, mid_gain[None, :], mid_bias[None, :]))
     triangle = call(
         functools.partial(product_kernel, order),
-        jax.ShapeDtypeStruct((len(order), 2, half, lanes), BF16),
+        jax.ShapeDtypeStruct((len(order), 2, half, lanes), F32),
         (),
         2 * 2 * (2 * count * half) * (4 * count * half) * depth,
     )(left, right, other)

time: 49.5 us -> 55.3 us (1.12)
  blocking collectives: 42.8 us -> 48.5 us
    all_to_all x2, blocking collectives: 42.8 us -> 48.5 us  [exchange(): lax.all_to_all(values, BOTH, 0, 0, axis_index_groups=devices, tiled=True)]
where the time goes in v9:
time: 55.3 us; the launch traced here: 55 us
  blocking collectives  48.5 us (88%)
  Pallas kernels  5.69 us (10%)
  waiting for transfers between devices  0.7 us (1%)
    all_to_all x2, blocking collectives, exchange(): lax.all_to_all(values, BOTH, 0, 0, axis_index_groups=devices, tiled=True)  48.5 us
    pallas_call x1, Pallas kernels, per_device(): call(operands_kernel, (jax.ShapeDtypeStruct((hidden, 2 * half, lanes), BF...  2.2 us
    pallas_call x1, Pallas kernels, per_device(): call(update_kernel, jax.ShapeDtypeStruct(pair.shape, BF16), [pltpu.VMEM((...  1.48 us
    pallas_call x1, Pallas kernels, per_device(): call(functools.partial(gate_kernel, order), (arranged, jax.ShapeDtypeStru...  1.19 us
  transfers between devices with their start and end apart: 1, of which 1 were waited for; matrix products, arithmetic and copies ran while one was open for 0% of the time, Pallas kernels for 2%

profile of v9, /device:TPU:0, one launch (start us, length us, event | category | flops | bytes accessed | tf_op | source)
XLA Modules:
  0.0 55.0 jit_solution(3256604147641588638)
XLA Ops:
  0.0 2.2 %shard_map.109 = (bf16[128,32,128]{2,1,0:T(8,128)(2,1)S(1)}, bf16[128,2048]{1,0:T(8,128)(2,1)S(1)}) custom-call(bf16[32,64,128]{2,1,0:T(8,128)(2,1)} %pair_hbm.1, f32[1,128]{1,0:T(1,128)} %bitcast.15, f32[1,128]{1,0:T(1,128)} %bitcast.16, bf16[128,128]{1,0:T(8,128)(2,1)} %ag_hbm.1, bf16[128,128]{1,0:T(8,128)(2,1)} %ap_hbm.1, bf16[128,128]{1,0:T(8,128)(2,1)} %bg_hbm.1, ...), custom_call_target="tpu_custom_call" | custom-call | flops 268435456 | bytes 1048576 | tf_op jit(solution)/shard_map/pallas_call | solution.py:198
  2.2 25.6 %all_to_all.10 = bf16[64,64,128]{2,1,0:T(8,128)(2,1)S(1)} all-to-all(bf16[64,64,128]{2,1,0:T(8,128)(2,1)S(1)} %bitcast.12), channel_id=1, replica_groups={{98,0,1,2,3,4,5,6,7,16,17,18,19,20,21,22,23,32,33,34,35,36,37,38,39,48,..., dimensions={0} | all-to-all | bytes 2097152 | tf_op jit(solution)/shard_map/all_to_all | solution.py:26
  27.8 0.2 shard_map.111.right_ref
  28.0 0.1 collective-permute-start
  28.1 1.2 %shard_map.110 = (bf16[2,8,2,16,512]{4,3,2,1,0:T(8,128)(2,1)S(1)}, f32[16,128,128]{2,1,0:T(8,128)S(1)}, f32[128,128]{1,0:T(8,128)S(1)}, f32[128,128]{1,0:T(8,128)S(1)}, bf16[128,128]{1,0:T(8,128)(2,1)S(1)}) custom-call(bf16[64,2,32,128]{3,2,1,0:T(8,128)(2,1)S(1)} %bitcast.9, bf16[128,2048]{1,0:T(8,128)(2,1)S(1)} %get-tuple-element.13.normed_ref, ...), custom_call_target="tpu_custom_call" | custom-call | bytes 1048576 | tf_op jit(solution)/shard_map/pallas_call | solution.py:222
  29.3 0.7 %collective-permute-done.other_ref = bf16[2,8,2,16,512]{4,3,2,1,0:T(8,128)(2,1)S(1)} collective-permute-done((bf16[2,8,2,16,512]{4,3,2,1,0:T(8,128)(2,1)S(1)}, bf16[2,8,2,16,512]{4,3,2,1,0:T(8,128)(2,1)S(1)}, u32[]{:S(2)}, u32[]{:S(2)}) %collective-permute-start) | collective-permute-done | bytes 524320 | tf_op jit(solution)/shard_map/ppermute | solution.py:220
  30.0 0.6 %shard_map.112 = f32[64,2,16,128]{3,2,1,0:T(8,128)S(1)} custom-call(bf16[2,8,2,16,512]{4,3,2,1,0:T(8,128)(2,1)S(1)} %get-tuple-element.14.left_ref, bf16[2,8,2,16,512]{4,3,2,1,0:T(8,128)(2,1)S(1)} %shard_map.111.right_ref, bf16[2,8,2,16,512]{4,3,2,1,0:T(8,128)(2,1)S(1)} %collective-permute-done.other_ref), custom_call_target="tpu_custom_call" | custom-call | flops 268435456 | bytes 1048576 | tf_op jit(solution)/shard_map/pallas_call | solution.py:238
  30.7 22.8 %all_to_all.11 = f32[64,32,128]{2,1,0:T(8,128)S(1)} all-to-all(f32[64,32,128]{2,1,0:T(8,128)S(1)} %bitcast.11), channel_id=1, replica_groups={{98,0,1,2,3,4,5,6,7,16,17,18,19,20,21,22,23,32,33,34,35,36,37,38,39,48,..., dimensions={0} | all-to-all | bytes 2097152 | tf_op jit(solution)/shard_map/all_to_all | solution.py:26
  53.5 1.5 %shard_map.113 = bf16[32,64,128]{2,1,0:T(8,128)(2,1)} custom-call(f32[128,16,128]{2,1,0:T(8,128)S(1)} %bitcast.10, f32[16,128,128]{2,1,0:T(8,128)S(1)} %get-tuple-element.15.gate_ref, f32[128,128]{1,0:T(8,128)S(1)} %get-tuple-element.16.gain_ref, f32[128,128]{1,0:T(8,128)S(1)} %get-tuple-element.17.bias_ref, bf16[128,128]{1,0:T(8,128)(2,1)S(1)} %get-tuple-element.18.weight_ref), custom_call_target="tpu_custom_call" | custom-call | flops 67108864 | bytes 1048576 | tf_op jit(solution)/shard_map/pallas_call | solution.py:246
Async XLA Ops:
  28.0 2.0 %collective-permute-start = (bf16[2,8,2,16,512]{4,3,2,1,0:T(8,128)(2,1)S(1)}, bf16[2,8,2,16,512]{4,3,2,1,0:T(8,128)(2,1)S(1)}, u32[]{:S(2)}, u32[]{:S(2)}) collective-permute-start(bf16[2,8,2,16,512]{4,3,2,1,0:T(8,128)(2,1)S(1)} %shard_map.111.right_ref), channel_id=1, source_target_pairs={{0,8},{8,0},{16,24},{24,16},{32,40},{40,32},{48,56},{56,48},{64,72... | collective-permute-start | bytes 1572872 | tf_op jit(solution)/shard_map/ppermute | solution.py:220

commit v10 on v8

--- a/solution.py
+++ b/solution.py
@@ -26,24 +26,12 @@
     return lax.all_to_all(values, BOTH, 0, 0, axis_index_groups=devices, tiled=True)
 
 
-def centring(size):
-    same = lax.broadcasted_iota(jnp.int32, (size, size), 0) == lax.broadcasted_iota(jnp.int32, (size, size), 1)
-    return jnp.where(same, 1 - 1 / size, -1 / size).astype(BF16)
-
-
 def dot(a, b, contract):
     return lax.dot_general(a, b, ((contract[:1], contract[1:]), ((), ())), preferred_element_type=F32)
 
 
 def column(vector, width):
     return jnp.broadcast_to(vector, (width, vector.shape[1])).T
-
-
-def norm(values, axis):
-    mean = jnp.mean(values, axis=axis, keepdims=True)
-    centered = values - mean
-    variance = jnp.mean(centered * centered, axis=axis, keepdims=True)
-    return centered * lax.rsqrt(variance + EPS)
 
 
 def start(copies):
@@ -72,11 +60,12 @@
     fetch.start()
     start(small)
     wait(small)
+    fetch.wait()
     weights = jnp.concatenate([weight_ref[n].T * jnp.asarray(0.5, BF16) for n in range(4)], axis=0)
     gain, bias = (jnp.concatenate([column(vector_ref[n : n + 1], LANES)] * half, axis=1) for n in range(2))
-    fetch.wait()
-    block = jnp.concatenate([pair_ref[row] for s in range(half) for row in (s, half + s)], axis=0)
-    centered = dot(centring(chans), block, (1, 1))
+    tiles = [jnp.concatenate([pair_ref[s], pair_ref[half + s]], axis=0).T for s in range(half)]
+    turned = jnp.concatenate(tiles, axis=1).astype(F32)
+    centered = turned - jnp.mean(turned, axis=0, keepdims=True)
     variance = jnp.mean(centered * centered, axis=0, keepdims=True)
     normed = (centered * lax.rsqrt(variance + EPS) * gain + bias).astype(BF16)
     normed_ref[...] = normed
@@ -150,13 +139,17 @@
     chans, half, lanes = in_ref.shape
     cols = lanes // 2
     pitch = half + 1
-    normed = norm(in_ref[...].astype(F32), 0)
+    values = in_ref[...].astype(F32)
     for c in range(chans):
-        wide_ref[pl.ds(c * pitch, half), :] = normed[c]
+        wide_ref[pl.ds(c * pitch, half), :] = values[c]
+    mean = jnp.mean(values, axis=0)
+    centered = values - mean
+    scale = lax.rsqrt(jnp.mean(centered * centered, axis=0) + EPS)
     step = half // PARTS
     copies = []
     for s in range(half):
-        mixed = (wide_ref[pl.ds(s, chans, stride=pitch), :] * gain_ref[...] + bias_ref[...]).astype(BF16)
+        values = (wide_ref[pl.ds(s, chans, stride=pitch), :] - mean[s : s + 1]) * scale[s : s + 1]
+        mixed = (values * gain_ref[...] + bias_ref[...]).astype(BF16)
         output = dot(mixed, weight_ref[...], (0, 0))
         update = (gate_ref[s] * output).astype(BF16)
         out_ref[s], out_ref[half + s] = update[:cols], update[cols:]

time: 49.5 us -> 49.5 us (level)
  no operation moved by 1% of the time
where the time goes in v10:
time: 49.5 us; the launch traced here: 49.2 us
  blocking collectives  42.8 us (86%)
  Pallas kernels  5.57 us (11%)
  waiting for transfers between devices  0.7 us (1%)
    all_to_all x2, blocking collectives, exchange(): lax.all_to_all(values, BOTH, 0, 0, axis_index_groups=devices, tiled=True)  42.8 us
    pallas_call x1, Pallas kernels, per_device(): call(operands_kernel, (jax.ShapeDtypeStruct((hidden, 2 * half, lanes), BF...  2.16 us
    pallas_call x1, Pallas kernels, per_device(): call(update_kernel, jax.ShapeDtypeStruct(pair.shape, BF16), [pltpu.VMEM((...  1.46 us
    pallas_call x1, Pallas kernels, per_device(): call(functools.partial(gate_kernel, order), (arranged, jax.ShapeDtypeStru...  1.19 us
  transfers between devices with their start and end apart: 1, of which 1 were waited for; matrix products, arithmetic and copies ran while one was open for 0% of the time, Pallas kernels for 2%

profile of v10, /device:TPU:0, one launch (start us, length us, event | category | flops | bytes accessed | tf_op | source)
XLA Modules:
  0.0 49.2 jit_solution(6918594884542129805)
XLA Ops:
  0.0 2.2 %shard_map.109 = (bf16[128,32,128]{2,1,0:T(8,128)(2,1)S(1)}, bf16[128,2048]{1,0:T(8,128)(2,1)S(1)}) custom-call(bf16[32,64,128]{2,1,0:T(8,128)(2,1)} %pair_hbm.1, f32[1,128]{1,0:T(1,128)} %bitcast.15, f32[1,128]{1,0:T(1,128)} %bitcast.16, bf16[128,128]{1,0:T(8,128)(2,1)} %ag_hbm.1, bf16[128,128]{1,0:T(8,128)(2,1)} %ap_hbm.1, bf16[128,128]{1,0:T(8,128)(2,1)} %bg_hbm.1, ...), custom_call_target="tpu_custom_call" | custom-call | flops 268435456 | bytes 1048576 | tf_op jit(solution)/shard_map/pallas_call | solution.py:191
  2.2 25.6 %all_to_all.10 = bf16[64,64,128]{2,1,0:T(8,128)(2,1)S(1)} all-to-all(bf16[64,64,128]{2,1,0:T(8,128)(2,1)S(1)} %bitcast.12), channel_id=1, replica_groups={{98,0,1,2,3,4,5,6,7,16,17,18,19,20,21,22,23,32,33,34,35,36,37,38,39,48,..., dimensions={0} | all-to-all | bytes 2097152 | tf_op jit(solution)/shard_map/all_to_all | solution.py:26
  27.8 0.2 shard_map.111.right_ref
  28.0 0.1 collective-permute-start
  28.1 1.2 %shard_map.110 = (bf16[2,8,2,16,512]{4,3,2,1,0:T(8,128)(2,1)S(1)}, f32[16,128,128]{2,1,0:T(8,128)S(1)}, f32[128,128]{1,0:T(8,128)S(1)}, f32[128,128]{1,0:T(8,128)S(1)}, bf16[128,128]{1,0:T(8,128)(2,1)S(1)}) custom-call(bf16[64,2,32,128]{3,2,1,0:T(8,128)(2,1)S(1)} %bitcast.9, bf16[128,2048]{1,0:T(8,128)(2,1)S(1)} %get-tuple-element.13.normed_ref, ...), custom_call_target="tpu_custom_call" | custom-call | bytes 1048576 | tf_op jit(solution)/shard_map/pallas_call | solution.py:215
  29.3 0.7 %collective-permute-done.other_ref = bf16[2,8,2,16,512]{4,3,2,1,0:T(8,128)(2,1)S(1)} collective-permute-done((bf16[2,8,2,16,512]{4,3,2,1,0:T(8,128)(2,1)S(1)}, bf16[2,8,2,16,512]{4,3,2,1,0:T(8,128)(2,1)S(1)}, u32[]{:S(2)}, u32[]{:S(2)}) %collective-permute-start) | collective-permute-done | bytes 524320 | tf_op jit(solution)/shard_map/ppermute | solution.py:213
  30.0 0.6 %shard_map.112 = bf16[64,2,16,128]{3,2,1,0:T(8,128)(2,1)S(1)} custom-call(bf16[2,8,2,16,512]{4,3,2,1,0:T(8,128)(2,1)S(1)} %get-tuple-element.14.left_ref, bf16[2,8,2,16,512]{4,3,2,1,0:T(8,128)(2,1)S(1)} %shard_map.111.right_ref, bf16[2,8,2,16,512]{4,3,2,1,0:T(8,128)(2,1)S(1)} %collective-permute-done.other_ref), custom_call_target="tpu_custom_call" | custom-call | flops 268435456 | bytes 1048576 | tf_op jit(solution)/shard_map/pallas_call | solution.py:231
  30.5 17.2 %all_to_all.11 = bf16[64,32,128]{2,1,0:T(8,128)(2,1)S(1)} all-to-all(bf16[64,32,128]{2,1,0:T(8,128)(2,1)S(1)} %bitcast.11), channel_id=1, replica_groups={{98,0,1,2,3,4,5,6,7,16,17,18,19,20,21,22,23,32,33,34,35,36,37,38,39,48,..., dimensions={0} | all-to-all | bytes 1048576 | tf_op jit(solution)/shard_map/all_to_all | solution.py:26
  47.7 1.5 %shard_map.113 = bf16[32,64,128]{2,1,0:T(8,128)(2,1)} custom-call(bf16[128,16,128]{2,1,0:T(8,128)(2,1)S(1)} %bitcast.10, f32[16,128,128]{2,1,0:T(8,128)S(1)} %get-tuple-element.15.gate_ref, f32[128,128]{1,0:T(8,128)S(1)} %get-tuple-element.16.gain_ref, f32[128,128]{1,0:T(8,128)S(1)} %get-tuple-element.17.bias_ref, ...), custom_call_target="tpu_custom_call" | custom-call | flops 67108864 | bytes 1048576 | tf_op jit(solution)/shard_map/pallas_call | solution.py:239
Async XLA Ops:
  28.0 2.0 %collective-permute-start = (bf16[2,8,2,16,512]{4,3,2,1,0:T(8,128)(2,1)S(1)}, bf16[2,8,2,16,512]{4,3,2,1,0:T(8,128)(2,1)S(1)}, u32[]{:S(2)}, u32[]{:S(2)}) collective-permute-start(bf16[2,8,2,16,512]{4,3,2,1,0:T(8,128)(2,1)S(1)} %shard_map.111.right_ref), channel_id=1, source_target_pairs={{0,8},{8,0},{16,24},{24,16},{32,40},{40,32},{48,56},{56,48},{64,72... | collective-permute-start | bytes 1572872 | tf_op jit(solution)/shard_map/ppermute | solution.py:213

commit v11 on v10

--- a/solution.py
+++ b/solution.py
@@ -47,7 +47,7 @@
 
 def operands_kernel(
     pair_hbm, gain_hbm, bias_hbm, ag_hbm, ap_hbm, bg_hbm, bp_hbm,
-    out_ref, normed_ref, pair_ref, vector_ref, weight_ref, wide_ref, sem,
+    out_ref, normed_ref, pair_ref, vector_ref, weight_ref, wide_ref, other_ref, sem,
 ):
     rows, _, chans = pair_hbm.shape
     half = rows // 2
@@ -72,13 +72,14 @@
     projected = dot(weights, normed, (1, 0))
     a_gate, a_proj, b_gate, b_proj = (projected[n * chans : (n + 1) * chans] for n in range(4))
     left, right = a_proj + jnp.tanh(a_gate) * a_proj, b_proj + jnp.tanh(b_gate) * b_proj
-    pitch = 2 * half + 1
+    pitch = half + 1
     for s in range(half):
         cut = slice(s * LANES, (s + 1) * LANES)
         wide_ref[pl.ds(s, chans, stride=pitch), :] = left[:, cut]
-        wide_ref[pl.ds(half + s, chans, stride=pitch), :] = right[:, cut]
+        other_ref[pl.ds(s, chans, stride=pitch), :] = right[:, cut]
     for c in range(chans):
-        out_ref[c] = wide_ref[pl.ds(c * pitch, 2 * half), :].astype(BF16)
+        out_ref[c, :half] = wide_ref[pl.ds(c * pitch, half), :].astype(BF16)
+        out_ref[c, half:] = other_ref[pl.ds(c * pitch, half), :].astype(BF16)
 
 
 def merge(even, odd, cols):
@@ -198,7 +199,8 @@
             pltpu.VMEM(pair.shape, BF16),
             pltpu.VMEM((8, chans), F32),
             pltpu.VMEM((4, chans, hidden), BF16),
-            pltpu.VMEM(((hidden + 8) * (2 * half + 1), lanes), F32),
+            pltpu.VMEM(((hidden + 8) * (half + 1), lanes), F32),
+            pltpu.VMEM(((hidden + 8) * (half + 1), lanes), F32),
             pltpu.SemaphoreType.DMA((7,)),
         ],
         2 * rows * cols * chans * 4 * hidden,

time: 49.5 us -> 49.4 us (level)
  no operation moved by 1% of the time
where the time goes in v11:
time: 49.4 us; the launch traced here: 49.2 us
  blocking collectives  42.8 us (87%)
  Pallas kernels  5.56 us (11%)
  waiting for transfers between devices  0.7 us (1%)
    all_to_all x2, blocking collectives, exchange(): lax.all_to_all(values, BOTH, 0, 0, axis_index_groups=devices, tiled=True)  42.8 us
    pallas_call x1, Pallas kernels, per_device(): call(operands_kernel, (jax.ShapeDtypeStruct((hidden, 2 * half, lanes), BF...  2.15 us
    pallas_call x1, Pallas kernels, per_device(): call(update_kernel, jax.ShapeDtypeStruct(pair.shape, BF16), [pltpu.VMEM((...  1.46 us
    pallas_call x1, Pallas kernels, per_device(): call(functools.partial(gate_kernel, order), (arranged, jax.ShapeDtypeStru...  1.19 us
  transfers between devices with their start and end apart: 1, of which 1 were waited for; matrix products, arithmetic and copies ran while one was open for 0% of the time, Pallas kernels for 2%

profile of v11, /device:TPU:0, one launch (start us, length us, event | category | flops | bytes accessed | tf_op | source)
XLA Modules:
  0.0 49.2 jit_solution(345000761303387396)
XLA Ops:
  0.0 2.1 %shard_map.109 = (bf16[128,32,128]{2,1,0:T(8,128)(2,1)S(1)}, bf16[128,2048]{1,0:T(8,128)(2,1)S(1)}) custom-call(bf16[32,64,128]{2,1,0:T(8,128)(2,1)} %pair_hbm.1, f32[1,128]{1,0:T(1,128)} %bitcast.15, f32[1,128]{1,0:T(1,128)} %bitcast.16, bf16[128,128]{1,0:T(8,128)(2,1)} %ag_hbm.1, bf16[128,128]{1,0:T(8,128)(2,1)} %ap_hbm.1, bf16[128,128]{1,0:T(8,128)(2,1)} %bg_hbm.1, ...), custom_call_target="tpu_custom_call" | custom-call | flops 268435456 | bytes 1048576 | tf_op jit(solution)/shard_map/pallas_call | solution.py:192
  2.2 25.6 %all_to_all.10 = bf16[64,64,128]{2,1,0:T(8,128)(2,1)S(1)} all-to-all(bf16[64,64,128]{2,1,0:T(8,128)(2,1)S(1)} %bitcast.12), channel_id=1, replica_groups={{98,0,1,2,3,4,5,6,7,16,17,18,19,20,21,22,23,32,33,34,35,36,37,38,39,48,..., dimensions={0} | all-to-all | bytes 2097152 | tf_op jit(solution)/shard_map/all_to_all | solution.py:26
  27.8 0.2 shard_map.111.right_ref
  28.0 0.1 collective-permute-start
  28.1 1.2 %shard_map.110 = (bf16[2,8,2,16,512]{4,3,2,1,0:T(8,128)(2,1)S(1)}, f32[16,128,128]{2,1,0:T(8,128)S(1)}, f32[128,128]{1,0:T(8,128)S(1)}, f32[128,128]{1,0:T(8,128)S(1)}, bf16[128,128]{1,0:T(8,128)(2,1)S(1)}) custom-call(bf16[64,2,32,128]{3,2,1,0:T(8,128)(2,1)S(1)} %bitcast.9, bf16[128,2048]{1,0:T(8,128)(2,1)S(1)} %get-tuple-element.13.normed_ref, ...), custom_call_target="tpu_custom_call" | custom-call | bytes 1048576 | tf_op jit(solution)/shard_map/pallas_call | solution.py:217
  29.3 0.7 %collective-permute-done.other_ref = bf16[2,8,2,16,512]{4,3,2,1,0:T(8,128)(2,1)S(1)} collective-permute-done((bf16[2,8,2,16,512]{4,3,2,1,0:T(8,128)(2,1)S(1)}, bf16[2,8,2,16,512]{4,3,2,1,0:T(8,128)(2,1)S(1)}, u32[]{:S(2)}, u32[]{:S(2)}) %collective-permute-start) | collective-permute-done | bytes 524320 | tf_op jit(solution)/shard_map/ppermute | solution.py:215
  30.0 0.6 %shard_map.112 = bf16[64,2,16,128]{3,2,1,0:T(8,128)(2,1)S(1)} custom-call(bf16[2,8,2,16,512]{4,3,2,1,0:T(8,128)(2,1)S(1)} %get-tuple-element.14.left_ref, bf16[2,8,2,16,512]{4,3,2,1,0:T(8,128)(2,1)S(1)} %shard_map.111.right_ref, bf16[2,8,2,16,512]{4,3,2,1,0:T(8,128)(2,1)S(1)} %collective-permute-done.other_ref), custom_call_target="tpu_custom_call" | custom-call | flops 268435456 | bytes 1048576 | tf_op jit(solution)/shard_map/pallas_call | solution.py:233
  30.5 17.2 %all_to_all.11 = bf16[64,32,128]{2,1,0:T(8,128)(2,1)S(1)} all-to-all(bf16[64,32,128]{2,1,0:T(8,128)(2,1)S(1)} %bitcast.11), channel_id=1, replica_groups={{98,0,1,2,3,4,5,6,7,16,17,18,19,20,21,22,23,32,33,34,35,36,37,38,39,48,..., dimensions={0} | all-to-all | bytes 1048576 | tf_op jit(solution)/shard_map/all_to_all | solution.py:26
  47.7 1.5 %shard_map.113 = bf16[32,64,128]{2,1,0:T(8,128)(2,1)} custom-call(bf16[128,16,128]{2,1,0:T(8,128)(2,1)S(1)} %bitcast.10, f32[16,128,128]{2,1,0:T(8,128)S(1)} %get-tuple-element.15.gate_ref, f32[128,128]{1,0:T(8,128)S(1)} %get-tuple-element.16.gain_ref, f32[128,128]{1,0:T(8,128)S(1)} %get-tuple-element.17.bias_ref, ...), custom_call_target="tpu_custom_call" | custom-call | flops 67108864 | bytes 1048576 | tf_op jit(solution)/shard_map/pallas_call | solution.py:241
Async XLA Ops:
  28.0 2.0 %collective-permute-start = (bf16[2,8,2,16,512]{4,3,2,1,0:T(8,128)(2,1)S(1)}, bf16[2,8,2,16,512]{4,3,2,1,0:T(8,128)(2,1)S(1)}, u32[]{:S(2)}, u32[]{:S(2)}) collective-permute-start(bf16[2,8,2,16,512]{4,3,2,1,0:T(8,128)(2,1)S(1)} %shard_map.111.right_ref), channel_id=1, source_target_pairs={{0,8},{8,0},{16,24},{24,16},{32,40},{40,32},{48,56},{56,48},{64,72... | collective-permute-start | bytes 1572872 | tf_op jit(solution)/shard_map/ppermute | solution.py:215

commit v12 on v10

--- a/solution.py
+++ b/solution.py
@@ -86,7 +86,8 @@
 
 
 def arrange_kernel(order, part, in_ref, out_ref):
-    channels, rows, _, tile, depth = out_ref.shape
+    channels, tile, depth = out_ref.shape[0], *out_ref.shape[3:]
+    rows = out_ref.shape[1 + (part == 0)]
     lanes = in_ref.shape[3]
     count = 2 * depth // lanes
     for channel in range(channels):
@@ -94,7 +95,8 @@
             tiles = [in_ref[order.index(row * count + col), channel, pl.ds(part * tile, tile), :] for col in range(count)]
             for m in range(count // 2):
                 for h, block in enumerate(merge(tiles[2 * m], tiles[2 * m + 1], lanes // 2)):
-                    out_ref[channel, row, h, :, m * lanes : (m + 1) * lanes] = block
+                    at = (h, row) if part == 0 else (row, h)
+                    out_ref[channel, *at, :, m * lanes : (m + 1) * lanes] = block
 
 
 def gate_kernel(
@@ -117,7 +119,7 @@
 
 
 def product_kernel(order, left_ref, right_ref, other_ref, out_ref):
-    channels, rows, _, tile, depth = left_ref.shape
+    channels, _, rows, tile, depth = left_ref.shape
     lanes = out_ref.shape[3]
     cols, count = lanes // 2, rows * tile
     core = lax.rem(lax.axis_index("row"), 2)
@@ -125,7 +127,7 @@
         own, other = right_ref[channel], other_ref[channel]
         right = jnp.stack([jnp.where(core == 0, own, other), jnp.where(core == 0, other, own)], axis=1)
         right = right.reshape(4 * count, depth)
-        left = jnp.concatenate([left_ref[channel, :, h].reshape(count, depth) for h in range(2)], axis=0)
+        left = left_ref[channel].reshape(2 * count, depth)
         product = dot(left, right, (1, 1)).astype(BF16)
         for m in range(4 * count // lanes):
             cut = slice(m * lanes, (m + 1) * lanes)
@@ -215,7 +217,7 @@
     left, gate, mid_gain, mid_bias, out_proj = call(
         functools.partial(gate_kernel, order),
         (
-            arranged,
+            jax.ShapeDtypeStruct((2, 2, count, half, depth), BF16),
             jax.ShapeDtypeStruct((half, lanes, chans), F32),
             late,
             late,

time: 49.5 us -> 49.5 us (level)
  no operation moved by 1% of the time
where the time goes in v12:
time: 49.5 us; the launch traced here: 49.2 us
  blocking collectives  42.8 us (86%)
  Pallas kernels  5.57 us (11%)
  waiting for transfers between devices  0.7 us (1%)
    all_to_all x2, blocking collectives, exchange(): lax.all_to_all(values, BOTH, 0, 0, axis_index_groups=devices, tiled=True)  42.8 us
    pallas_call x1, Pallas kernels, per_device(): call(operands_kernel, (jax.ShapeDtypeStruct((hidden, 2 * half, lanes), BF...  2.16 us
    pallas_call x1, Pallas kernels, per_device(): call(update_kernel, jax.ShapeDtypeStruct(pair.shape, BF16), [pltpu.VMEM((...  1.46 us
    pallas_call x1, Pallas kernels, per_device(): call(functools.partial(gate_kernel, order), (jax.ShapeDtypeStruct((2, 2,...  1.19 us
  transfers between devices with their start and end apart: 1, of which 1 were waited for; matrix products, arithmetic and copies ran while one was open for 0% of the time, Pallas kernels for 2%

profile of v12, /device:TPU:0, one launch (start us, length us, event | category | flops | bytes accessed | tf_op | source)
XLA Modules:
  0.0 49.2 jit_solution(7870169328707681064)
XLA Ops:
  0.0 2.2 %shard_map.109 = (bf16[128,32,128]{2,1,0:T(8,128)(2,1)S(1)}, bf16[128,2048]{1,0:T(8,128)(2,1)S(1)}) custom-call(bf16[32,64,128]{2,1,0:T(8,128)(2,1)} %pair_hbm.1, f32[1,128]{1,0:T(1,128)} %bitcast.15, f32[1,128]{1,0:T(1,128)} %bitcast.16, bf16[128,128]{1,0:T(8,128)(2,1)} %ag_hbm.1, bf16[128,128]{1,0:T(8,128)(2,1)} %ap_hbm.1, bf16[128,128]{1,0:T(8,128)(2,1)} %bg_hbm.1, ...), custom_call_target="tpu_custom_call" | custom-call | flops 268435456 | bytes 1048576 | tf_op jit(solution)/shard_map/pallas_call | solution.py:193
  2.2 25.6 %all_to_all.10 = bf16[64,64,128]{2,1,0:T(8,128)(2,1)S(1)} all-to-all(bf16[64,64,128]{2,1,0:T(8,128)(2,1)S(1)} %bitcast.12), channel_id=1, replica_groups={{98,0,1,2,3,4,5,6,7,16,17,18,19,20,21,22,23,32,33,34,35,36,37,38,39,48,..., dimensions={0} | all-to-all | bytes 2097152 | tf_op jit(solution)/shard_map/all_to_all | solution.py:26
  27.8 0.2 shard_map.111.right_ref
  28.0 0.1 collective-permute-start
  28.1 1.2 %shard_map.110 = (bf16[2,2,8,16,512]{4,3,2,1,0:T(8,128)(2,1)S(1)}, f32[16,128,128]{2,1,0:T(8,128)S(1)}, f32[128,128]{1,0:T(8,128)S(1)}, f32[128,128]{1,0:T(8,128)S(1)}, bf16[128,128]{1,0:T(8,128)(2,1)S(1)}) custom-call(bf16[64,2,32,128]{3,2,1,0:T(8,128)(2,1)S(1)} %bitcast.9, bf16[128,2048]{1,0:T(8,128)(2,1)S(1)} %get-tuple-element.13.normed_ref, ...), custom_call_target="tpu_custom_call" | custom-call | bytes 1048576 | tf_op jit(solution)/shard_map/pallas_call | solution.py:217
  29.3 0.7 %collective-permute-done.other_ref = bf16[2,8,2,16,512]{4,3,2,1,0:T(8,128)(2,1)S(1)} collective-permute-done((bf16[2,8,2,16,512]{4,3,2,1,0:T(8,128)(2,1)S(1)}, bf16[2,8,2,16,512]{4,3,2,1,0:T(8,128)(2,1)S(1)}, u32[]{:S(2)}, u32[]{:S(2)}) %collective-permute-start) | collective-permute-done | bytes 524320 | tf_op jit(solution)/shard_map/ppermute | solution.py:215
  30.0 0.6 %shard_map.112 = bf16[64,2,16,128]{3,2,1,0:T(8,128)(2,1)S(1)} custom-call(bf16[2,2,8,16,512]{4,3,2,1,0:T(8,128)(2,1)S(1)} %get-tuple-element.14.left_ref, bf16[2,8,2,16,512]{4,3,2,1,0:T(8,128)(2,1)S(1)} %shard_map.111.right_ref, bf16[2,8,2,16,512]{4,3,2,1,0:T(8,128)(2,1)S(1)} %collective-permute-done.other_ref), custom_call_target="tpu_custom_call" | custom-call | flops 268435456 | bytes 1048576 | tf_op jit(solution)/shard_map/pallas_call | solution.py:233
  30.5 17.2 %all_to_all.11 = bf16[64,32,128]{2,1,0:T(8,128)(2,1)S(1)} all-to-all(bf16[64,32,128]{2,1,0:T(8,128)(2,1)S(1)} %bitcast.11), channel_id=1, replica_groups={{98,0,1,2,3,4,5,6,7,16,17,18,19,20,21,22,23,32,33,34,35,36,37,38,39,48,..., dimensions={0} | all-to-all | bytes 1048576 | tf_op jit(solution)/shard_map/all_to_all | solution.py:26
  47.7 1.5 %shard_map.113 = bf16[32,64,128]{2,1,0:T(8,128)(2,1)} custom-call(bf16[128,16,128]{2,1,0:T(8,128)(2,1)S(1)} %bitcast.10, f32[16,128,128]{2,1,0:T(8,128)S(1)} %get-tuple-element.15.gate_ref, f32[128,128]{1,0:T(8,128)S(1)} %get-tuple-element.16.gain_ref, f32[128,128]{1,0:T(8,128)S(1)} %get-tuple-element.17.bias_ref, ...), custom_call_target="tpu_custom_call" | custom-call | flops 67108864 | bytes 1048576 | tf_op jit(solution)/shard_map/pallas_call | solution.py:241
Async XLA Ops:
  28.0 2.0 %collective-permute-start = (bf16[2,8,2,16,512]{4,3,2,1,0:T(8,128)(2,1)S(1)}, bf16[2,8,2,16,512]{4,3,2,1,0:T(8,128)(2,1)S(1)}, u32[]{:S(2)}, u32[]{:S(2)}) collective-permute-start(bf16[2,8,2,16,512]{4,3,2,1,0:T(8,128)(2,1)S(1)} %shard_map.111.right_ref), channel_id=1, source_target_pairs={{0,8},{8,0},{16,24},{24,16},{32,40},{40,32},{48,56},{56,48},{64,72... | collective-permute-start | bytes 1572872 | tf_op jit(solution)/shard_map/ppermute | solution.py:215

commit v13 on v10

--- a/solution.py
+++ b/solution.py
@@ -161,7 +161,7 @@
 
 
 LANES = 128
-PARTS = 4
+PARTS = 2
 VMEM_LIMIT = 48 * 2**20
 
 

time: 49.5 us -> 49.5 us (level)
  no operation moved by 1% of the time
where the time goes in v13:
time: 49.5 us; the launch traced here: 49.2 us
  blocking collectives  42.8 us (86%)
  Pallas kernels  5.59 us (11%)
  waiting for transfers between devices  0.7 us (1%)
    all_to_all x2, blocking collectives, exchange(): lax.all_to_all(values, BOTH, 0, 0, axis_index_groups=devices, tiled=True)  42.8 us
    pallas_call x1, Pallas kernels, per_device(): call(operands_kernel, (jax.ShapeDtypeStruct((hidden, 2 * half, lanes), BF...  2.16 us
    pallas_call x1, Pallas kernels, per_device(): call(update_kernel, jax.ShapeDtypeStruct(pair.shape, BF16), [pltpu.VMEM((...  1.47 us
    pallas_call x1, Pallas kernels, per_device(): call(functools.partial(gate_kernel, order), (arranged, jax.ShapeDtypeStru...  1.19 us
  transfers between devices with their start and end apart: 1, of which 1 were waited for; matrix products, arithmetic and copies ran while one was open for 0% of the time, Pallas kernels for 2%

profile of v13, /device:TPU:0, one launch (start us, length us, event | category | flops | bytes accessed | tf_op | source)
XLA Modules:
  0.0 49.2 jit_solution(17343616160024959455)
XLA Ops:
  0.0 2.2 %shard_map.109 = (bf16[128,32,128]{2,1,0:T(8,128)(2,1)S(1)}, bf16[128,2048]{1,0:T(8,128)(2,1)S(1)}) custom-call(bf16[32,64,128]{2,1,0:T(8,128)(2,1)} %pair_hbm.1, f32[1,128]{1,0:T(1,128)} %bitcast.15, f32[1,128]{1,0:T(1,128)} %bitcast.16, bf16[128,128]{1,0:T(8,128)(2,1)} %ag_hbm.1, bf16[128,128]{1,0:T(8,128)(2,1)} %ap_hbm.1, bf16[128,128]{1,0:T(8,128)(2,1)} %bg_hbm.1, ...), custom_call_target="tpu_custom_call" | custom-call | flops 268435456 | bytes 1048576 | tf_op jit(solution)/shard_map/pallas_call | solution.py:191
  2.2 25.6 %all_to_all.10 = bf16[64,64,128]{2,1,0:T(8,128)(2,1)S(1)} all-to-all(bf16[64,64,128]{2,1,0:T(8,128)(2,1)S(1)} %bitcast.12), channel_id=1, replica_groups={{98,0,1,2,3,4,5,6,7,16,17,18,19,20,21,22,23,32,33,34,35,36,37,38,39,48,..., dimensions={0} | all-to-all | bytes 2097152 | tf_op jit(solution)/shard_map/all_to_all | solution.py:26
  27.8 0.2 shard_map.111.right_ref
  28.0 0.1 collective-permute-start
  28.1 1.2 %shard_map.110 = (bf16[2,8,2,16,512]{4,3,2,1,0:T(8,128)(2,1)S(1)}, f32[16,128,128]{2,1,0:T(8,128)S(1)}, f32[128,128]{1,0:T(8,128)S(1)}, f32[128,128]{1,0:T(8,128)S(1)}, bf16[128,128]{1,0:T(8,128)(2,1)S(1)}) custom-call(bf16[64,2,32,128]{3,2,1,0:T(8,128)(2,1)S(1)} %bitcast.9, bf16[128,2048]{1,0:T(8,128)(2,1)S(1)} %get-tuple-element.13.normed_ref, ...), custom_call_target="tpu_custom_call" | custom-call | bytes 1048576 | tf_op jit(solution)/shard_map/pallas_call | solution.py:215
  29.3 0.7 %collective-permute-done.other_ref = bf16[2,8,2,16,512]{4,3,2,1,0:T(8,128)(2,1)S(1)} collective-permute-done((bf16[2,8,2,16,512]{4,3,2,1,0:T(8,128)(2,1)S(1)}, bf16[2,8,2,16,512]{4,3,2,1,0:T(8,128)(2,1)S(1)}, u32[]{:S(2)}, u32[]{:S(2)}) %collective-permute-start) | collective-permute-done | bytes 524320 | tf_op jit(solution)/shard_map/ppermute | solution.py:213
  30.0 0.6 %shard_map.112 = bf16[64,2,16,128]{3,2,1,0:T(8,128)(2,1)S(1)} custom-call(bf16[2,8,2,16,512]{4,3,2,1,0:T(8,128)(2,1)S(1)} %get-tuple-element.14.left_ref, bf16[2,8,2,16,512]{4,3,2,1,0:T(8,128)(2,1)S(1)} %shard_map.111.right_ref, bf16[2,8,2,16,512]{4,3,2,1,0:T(8,128)(2,1)S(1)} %collective-permute-done.other_ref), custom_call_target="tpu_custom_call" | custom-call | flops 268435456 | bytes 1048576 | tf_op jit(solution)/shard_map/pallas_call | solution.py:231
  30.5 17.2 %all_to_all.11 = bf16[64,32,128]{2,1,0:T(8,128)(2,1)S(1)} all-to-all(bf16[64,32,128]{2,1,0:T(8,128)(2,1)S(1)} %bitcast.11), channel_id=1, replica_groups={{98,0,1,2,3,4,5,6,7,16,17,18,19,20,21,22,23,32,33,34,35,36,37,38,39,48,..., dimensions={0} | all-to-all | bytes 1048576 | tf_op jit(solution)/shard_map/all_to_all | solution.py:26
  47.7 1.5 %shard_map.113 = bf16[32,64,128]{2,1,0:T(8,128)(2,1)} custom-call(bf16[128,16,128]{2,1,0:T(8,128)(2,1)S(1)} %bitcast.10, f32[16,128,128]{2,1,0:T(8,128)S(1)} %get-tuple-element.15.gate_ref, f32[128,128]{1,0:T(8,128)S(1)} %get-tuple-element.16.gain_ref, f32[128,128]{1,0:T(8,128)S(1)} %get-tuple-element.17.bias_ref, ...), custom_call_target="tpu_custom_call" | custom-call | flops 67108864 | bytes 1048576 | tf_op jit(solution)/shard_map/pallas_call | solution.py:239
Async XLA Ops:
  28.0 2.0 %collective-permute-start = (bf16[2,8,2,16,512]{4,3,2,1,0:T(8,128)(2,1)S(1)}, bf16[2,8,2,16,512]{4,3,2,1,0:T(8,128)(2,1)S(1)}, u32[]{:S(2)}, u32[]{:S(2)}) collective-permute-start(bf16[2,8,2,16,512]{4,3,2,1,0:T(8,128)(2,1)S(1)} %shard_map.111.right_ref), channel_id=1, source_target_pairs={{0,8},{8,0},{16,24},{24,16},{32,40},{40,32},{48,56},{56,48},{64,72... | collective-permute-start | bytes 1572872 | tf_op jit(solution)/shard_map/ppermute | solution.py:213
